TPU v7x, 32 devices: a whole 2x2x4 slice. The times are simulated.
32 devices in a mesh: seq: 2 (over x), dp: 16 (over z, y, core).
Axes of the slice: x: 2, y: 2, z: 4, core: 2. Of those that a mesh axis runs over, the one named last changes fastest.
Arguments:
- tokens: bfloat16 [16, 1024, 768], P('dp', 'seq'), may hold values from -6 to 6
- cotangent: bfloat16 [16, 1024, 768], P('dp', 'seq'), may hold values from -6 to 6
- attn_weight: bfloat16 [768, 3072], P('dp'), may hold values from -0.21875 to 0.21875
- mlp_weight: bfloat16 [2, 768, 3072], P(None, 'dp'), may hold values from -0.21650635 to 0.21650635
- norms: bfloat16 [4, 768], P(None, 'dp'), may hold values from -1 to 1.5
- taps: bfloat16 [64, 768], P(None, 'dp'), may hold values from -0.375 to 0.375
- ssm_params: float32 [2, 768, 64], P(None, 'seq'), may hold values from -10 to 0.15309311, as said below
- attn_moments: float32 [2, 768, 3072], P(None, 'dp'), may hold values from -1.5 to 2, as said below
- mlp_moments: float32 [2, 2, 768, 3072], P(None, None, 'dp'), may hold values from -1.5 to 2, as said below
- norm_moments: float32 [2, 4, 768], P(None, None, 'dp'), may hold values from -1.5 to 2, as said below
- tap_moments: float32 [2, 64, 768], P(None, None, 'dp'), may hold values from -1.5 to 2, as said below
- ssm_moments: float32 [2, 2, 768, 64], P(None, None, 'seq'), may hold values from -1.5 to 2, as said below
Outputs:
- layer_out: bfloat16 [16, 1024, 768], P('dp', 'seq')
- input_grad: float32 [16, 1024, 768], P('dp', 'seq')
- attn_step: float32 [768, 3072], P('dp')
- attn_moments_new: float32 [2, 768, 3072], P(None, 'dp')
- mlp_step: float32 [2, 768, 3072], P(None, 'dp')
- mlp_moments_new: float32 [2, 2, 768, 3072], P(None, None, 'dp')
- norms_step: float32 [4, 768], P(None, 'dp')
- norm_moments_new: float32 [2, 4, 768], P(None, None, 'dp')
- taps_step: float32 [64, 768], P(None, 'dp')
- tap_moments_new: float32 [2, 64, 768], P(None, None, 'dp')
- ssm_step: float32 [2, 768, 64], P(None, 'seq')
- ssm_moments_new: float32 [2, 2, 768, 64], P(None, None, 'seq')
Inputs may be any that keep to these rules, and one draw needn't show every extreme that they name: ssm_params[0] holds log rates from -10 to -3.5; ssm_params[1] holds coefficients. `attn_moments`: the second moments are positive. `mlp_moments`: the second moments are positive. `norm_moments`: the second moments are positive. `tap_moments`: the second moments are positive. `ssm_moments`: the second moments are positive.
All inputs are finite; a program needn't handle non-finite values.
Results may differ from a plain program's by a relative error of at most 0.01.
Values may be sent and summed in bfloat16 or wider, within the bound.
A program may use at most 320 MiB of HBM per device.

v0:
```python
from functools import partial
import math

import jax
import jax.numpy as jnp
import ml_dtypes
import numpy as np
from jax import lax
from jax.experimental import pallas as pl
from jax.experimental.pallas import tpu as pltpu
from jax.sharding import PartitionSpec as P

DFT_ROWS = 256


EPS_NORM = 1e-05
BETA_ONE = 0.9
BETA_TWO = 0.999
ADAM_EPS = 1e-08
LEARN_RATE = 0.001
SSM_LEARN_RATE = 0.00025
DECAY_RATE = 0.1
STEP_COUNT = 10.0
HIGHEST = lax.Precision.HIGHEST


def from_behind(block, axis, distance):
    devices = range(lax.axis_size(axis))
    route = [(i - distance, i) for i in devices if i - distance in devices]
    return lax.ppermute(block, axis, route)


def as_sent(value):

    def short(part):
        return part.astype(jnp.bfloat16) if part.dtype == jnp.float32 else part

    return jax.tree.map(short, value)


def layer_norm(values, gain_row, bias_row):
    average = jnp.mean(values, axis=-1, keepdims=True)
    centred = values - average
    variance = jnp.mean(centred * centred, axis=-1, keepdims=True)
    return centred * lax.rsqrt(variance + EPS_NORM) * gain_row + bias_row


def shift_mix(rim_rows, keys_part, taps_full):
    tap_count = taps_full.shape[0]
    row_count = keys_part.shape[0]
    extended = jnp.concatenate([rim_rows, keys_part], axis=0)
    summed = jnp.zeros_like(keys_part)
    for tap_index in range(tap_count):
        begin_row = tap_count - 1 - tap_index
        summed = summed + taps_full[tap_index] * extended[begin_row : begin_row + row_count]
    return summed


def kernel_rows(length_total, ssm_full):
    inner_count = math.gcd(length_total, 128)
    outer_count = length_total // inner_count
    decay_rates = jnp.exp(ssm_full[0])
    outer_offsets = (jnp.arange(outer_count) * inner_count).astype(jnp.float32)
    inner_offsets = jnp.arange(inner_count).astype(jnp.float32)
    outer_part = ssm_full[1][:, :, None] * jnp.exp(
        -decay_rates[:, :, None] * outer_offsets[None, None, :]
    )
    inner_part = jnp.exp(-decay_rates[:, :, None] * inner_offsets[None, None, :])
    kernel = jnp.einsum("cna,cnb->cab", outer_part, inner_part, precision=HIGHEST)
    return kernel.reshape(kernel.shape[0], length_total)


def dft_tables(length_total, first_count):
    full_length = 2 * length_total
    col_count = full_length // first_count
    half_rows = first_count // 2
    row_index = jnp.arange(half_rows, dtype=jnp.int32)
    freq_index = jnp.arange(first_count, dtype=jnp.int32)
    col_index = jnp.arange(col_count, dtype=jnp.int32)
    angle_first = (
        2.0
        * math.pi
        / first_count
        * (row_index[:, None] * freq_index[None, :] % first_count).astype(jnp.float32)
    )
    angle_twist = (
        2.0 * math.pi / full_length * (freq_index[:, None] * col_index[None, :]).astype(jnp.float32)
    )
    angle_last = (
        2.0
        * math.pi
        / col_count
        * (col_index[:, None] * col_index[None, :] % col_count).astype(jnp.float32)
    )
    return (
        jnp.cos(angle_first),
        jnp.sin(angle_first),
        jnp.cos(angle_twist),
        jnp.sin(angle_twist),
        jnp.cos(angle_last),
        jnp.sin(angle_last),
    )


def forward_dft(signal, tables):
    cos_first, sin_first, cos_twist, sin_twist, cos_last, sin_last = tables
    half_rows = cos_first.shape[0]
    col_count = cos_last.shape[0]
    folded = signal.reshape(signal.shape[0], half_rows, col_count)
    real_first = jnp.einsum("cmp,mk->ckp", folded, cos_first, precision=HIGHEST)
    imaginary_first = -jnp.einsum("cmp,mk->ckp", folded, sin_first, precision=HIGHEST)
    real_twist = real_first * cos_twist + imaginary_first * sin_twist
    imaginary_twist = imaginary_first * cos_twist - real_first * sin_twist
    real_last = jnp.einsum("ckp,pq->ckq", real_twist, cos_last, precision=HIGHEST) + jnp.einsum(
        "ckp,pq->ckq", imaginary_twist, sin_last, precision=HIGHEST
    )
    imaginary_last = jnp.einsum(
        "ckp,pq->ckq", imaginary_twist, cos_last, precision=HIGHEST
    ) - jnp.einsum("ckp,pq->ckq", real_twist, sin_last, precision=HIGHEST)
    return (real_last, imaginary_last)


def inverse_dft(spectrum, tables):
    cos_first, sin_first, cos_twist, sin_twist, cos_last, sin_last = tables
    real_part, imaginary_part = spectrum
    full_length = cos_first.shape[1] * cos_last.shape[0]
    real_inner = jnp.einsum("ckq,qp->ckp", real_part, cos_last, precision=HIGHEST) - jnp.einsum(
        "ckq,qp->ckp", imaginary_part, sin_last, precision=HIGHEST
    )
    imaginary_inner = jnp.einsum(
        "ckq,qp->ckp", imaginary_part, cos_last, precision=HIGHEST
    ) + jnp.einsum("ckq,qp->ckp", real_part, sin_last, precision=HIGHEST)
    real_twist = real_inner * cos_twist - imaginary_inner * sin_twist
    imaginary_twist = imaginary_inner * cos_twist + real_inner * sin_twist
    signal = jnp.einsum("ckp,mk->cmp", real_twist, cos_first, precision=HIGHEST) - jnp.einsum(
        "ckp,mk->cmp", imaginary_twist, sin_first, precision=HIGHEST
    )
    return signal.reshape(signal.shape[0], signal.shape[1] * signal.shape[2]) / full_length


def complex_product(left, right, conjugate_left):
    left_real, left_imaginary = left
    right_real, right_imaginary = right
    if conjugate_left:
        return (
            left_real * right_real + left_imaginary * right_imaginary,
            left_real * right_imaginary - left_imaginary * right_real,
        )
    return (
        left_real * right_real - left_imaginary * right_imaginary,
        left_real * right_imaginary + left_imaginary * right_real,
    )


def adam_update(param_now, moments, gradient, learn_rate, decay_weight):
    first_new = BETA_ONE * moments[0] + (1.0 - BETA_ONE) * gradient
    second_new = BETA_TWO * moments[1] + (1.0 - BETA_TWO) * gradient * gradient
    first_hat = first_new / (1.0 - BETA_ONE**STEP_COUNT)
    second_hat = second_new / (1.0 - BETA_TWO**STEP_COUNT)
    step_size = learn_rate * (
        first_hat / (jnp.sqrt(second_hat) + ADAM_EPS) + decay_weight * param_now
    )
    return (step_size, jnp.stack([first_new, second_new]))


def per_device(
    tokens,
    cotangent,
    attn_weight,
    mlp_weight,
    norms,
    taps,
    ssm_params,
    attn_moments,
    mlp_moments,
    norm_moments,
    tap_moments,
    ssm_moments,
):
    row_count = tokens.shape[1]
    model_width = tokens.shape[2]
    group_count = lax.axis_size("seq")
    owner_count = lax.axis_size("dp")
    length_total = row_count * group_count
    attn_full, mlp_full, norm_full, taps_full = (
        lax.all_gather(attn_weight, "dp", axis=0, tiled=True),
        lax.all_gather(mlp_weight, "dp", axis=1, tiled=True),
        lax.all_gather(norms, "dp", axis=1, tiled=True),
        lax.all_gather(taps, "dp", axis=1, tiled=True),
    )
    inputs = tokens[0].astype(jnp.float32)
    cot_rows = cotangent[0].astype(jnp.float32)
    norm_values = norm_full.astype(jnp.float32)
    taps_values = taps_full.astype(jnp.float32)
    tap_count = taps_values.shape[0]
    normed, norm_pull = jax.vjp(layer_norm, inputs, norm_values[0], norm_values[1])
    normed_low = normed.astype(jnp.bfloat16)
    project = jnp.dot(
        normed_low, attn_full[:, : 3 * model_width], preferred_element_type=jnp.float32
    )
    queries = project[:, :model_width]
    keys_part = project[:, model_width : 2 * model_width]
    values = project[:, 2 * model_width :]
    rim_rows = from_behind(
        keys_part[row_count - tap_count + 1 :].astype(jnp.bfloat16), "seq", 1
    ).astype(jnp.float32)
    shifted, shift_pull = jax.vjp(shift_mix, rim_rows, keys_part, taps_values)
    mixed_rows = (shifted * values).astype(jnp.bfloat16)
    moved_in = lax.all_to_all(mixed_rows.T, "seq", split_axis=0, concat_axis=1, tiled=True).astype(
        jnp.float32
    )
    tables = dft_tables(length_total, DFT_ROWS)
    kernel, kernel_pull = jax.vjp(partial(kernel_rows, length_total), ssm_params)
    kernel_freq = forward_dft(kernel, tables)
    input_freq = forward_dft(moved_in, tables)
    conv_channels = inverse_dft(complex_product(input_freq, kernel_freq, False), tables)
    conv_back = lax.all_to_all(
        conv_channels.astype(jnp.bfloat16), "seq", split_axis=1, concat_axis=0, tiled=True
    )
    conv_rows = conv_back.T.astype(jnp.float32)
    gated_rows = (queries * conv_rows).astype(jnp.bfloat16)
    branch = jnp.dot(
        gated_rows, attn_full[:, 3 * model_width :], preferred_element_type=jnp.float32
    )
    residual_one = inputs + branch
    normed_two, norm_two_pull = jax.vjp(layer_norm, residual_one, norm_values[2], norm_values[3])
    normed_two_low = normed_two.astype(jnp.bfloat16)
    before = jnp.dot(normed_two_low, mlp_full[0], preferred_element_type=jnp.float32)
    active, gelu_pull = jax.vjp(jax.nn.gelu, before)
    active_low = active.astype(jnp.bfloat16)
    mlp_out = jnp.einsum("tf,df->td", active_low, mlp_full[1], preferred_element_type=jnp.float32)
    layer_out = (residual_one + mlp_out).astype(jnp.bfloat16)
    attn_back, mlp_back = (
        lax.all_gather(attn_weight, "dp", axis=0, tiled=True),
        lax.all_gather(mlp_weight, "dp", axis=1, tiled=True),
    )
    grad_after = cotangent[0]
    grad_active = jnp.dot(grad_after, mlp_back[1], preferred_element_type=jnp.float32)
    grad_down = jnp.einsum("td,tf->df", grad_after, active_low, preferred_element_type=jnp.float32)
    grad_before = gelu_pull(grad_active)[0].astype(jnp.bfloat16)
    grad_up = jnp.einsum(
        "td,tf->df", normed_two_low, grad_before, preferred_element_type=jnp.float32
    )
    grad_normed_two = jnp.einsum(
        "tf,df->td", grad_before, mlp_back[0], preferred_element_type=jnp.float32
    )
    grad_residual_part, grad_gain_two, grad_bias_two = norm_two_pull(grad_normed_two)
    grad_residual = cot_rows + grad_residual_part
    grad_branch = grad_residual.astype(jnp.bfloat16)
    grad_out = jnp.einsum("td,te->de", gated_rows, grad_branch, preferred_element_type=jnp.float32)
    grad_gated = jnp.einsum(
        "te,de->td",
        grad_branch,
        attn_back[:, 3 * model_width :],
        preferred_element_type=jnp.float32,
    )
    grad_queries = grad_gated * conv_rows
    grad_conv = (grad_gated * queries).astype(jnp.bfloat16)
    grad_moved = lax.all_to_all(grad_conv.T, "seq", split_axis=0, concat_axis=1, tiled=True).astype(
        jnp.float32
    )
    grad_freq = forward_dft(grad_moved, tables)
    grad_input = inverse_dft(complex_product(kernel_freq, grad_freq, True), tables)
    grad_kernel = inverse_dft(complex_product(input_freq, grad_freq, True), tables)
    grad_ssm_local = kernel_pull(grad_kernel)[0]
    grad_ssm = lax.psum(grad_ssm_local, "dp")
    grad_mixed_back = lax.all_to_all(
        grad_input.astype(jnp.bfloat16), "seq", split_axis=1, concat_axis=0, tiled=True
    )
    grad_mixed = grad_mixed_back.T.astype(jnp.float32)
    grad_shifted = grad_mixed * values
    grad_values = grad_mixed * shifted
    grad_rim, grad_keys, grad_taps = shift_pull(grad_shifted)
    returned = from_behind(as_sent(grad_rim), "seq", -1).astype(grad_rim.dtype)
    grad_keys = grad_keys + jnp.pad(returned, ((row_count - tap_count + 1, 0), (0, 0)))
    grad_project = jnp.concatenate([grad_queries, grad_keys, grad_values], axis=1).astype(
        jnp.bfloat16
    )
    grad_qkv = jnp.einsum("td,te->de", normed_low, grad_project, preferred_element_type=jnp.float32)
    grad_normed = jnp.einsum(
        "te,de->td",
        grad_project,
        attn_back[:, : 3 * model_width],
        preferred_element_type=jnp.float32,
    )
    grad_input_part, grad_gain_one, grad_bias_one = norm_pull(grad_normed)
    input_grad = grad_residual + grad_input_part
    grad_attn = jnp.concatenate([grad_qkv, grad_out], axis=1)
    grad_mlp = jnp.stack([grad_up, grad_down])
    grad_norms = jnp.stack([grad_gain_one, grad_bias_one, grad_gain_two, grad_bias_two])
    owned_part = (
        lax.psum_scatter(
            grad_attn.astype(jnp.bfloat16), "dp", scatter_dimension=0, tiled=True
        ).astype(jnp.float32),
        lax.psum_scatter(
            grad_mlp.astype(jnp.bfloat16), "dp", scatter_dimension=1, tiled=True
        ).astype(jnp.float32),
        lax.psum_scatter(
            grad_norms.astype(jnp.bfloat16), "dp", scatter_dimension=1, tiled=True
        ).astype(jnp.float32),
        lax.psum_scatter(
            grad_taps.astype(jnp.bfloat16), "dp", scatter_dimension=1, tiled=True
        ).astype(jnp.float32),
    )
    summed = (
        lax.psum(owned_part[0].astype(jnp.bfloat16), "seq").astype(jnp.float32),
        lax.psum(owned_part[1].astype(jnp.bfloat16), "seq").astype(jnp.float32),
        lax.psum(owned_part[2].astype(jnp.bfloat16), "seq").astype(jnp.float32),
        lax.psum(owned_part[3].astype(jnp.bfloat16), "seq").astype(jnp.float32),
    )
    grad_scale = 1.0 / math.sqrt(owner_count * length_total)
    attn_step, attn_moments_new = adam_update(
        attn_weight.astype(jnp.float32),
        attn_moments,
        summed[0] * grad_scale,
        LEARN_RATE,
        DECAY_RATE,
    )
    mlp_step, mlp_moments_new = adam_update(
        mlp_weight.astype(jnp.float32), mlp_moments, summed[1] * grad_scale, LEARN_RATE, DECAY_RATE
    )
    norms_step, norm_moments_new = adam_update(
        norms.astype(jnp.float32), norm_moments, summed[2] * grad_scale, LEARN_RATE, 0.0
    )
    taps_step, tap_moments_new = adam_update(
        taps.astype(jnp.float32), tap_moments, summed[3] * grad_scale, LEARN_RATE, DECAY_RATE
    )
    ssm_step, ssm_moments_new = adam_update(
        ssm_params, ssm_moments, grad_ssm * grad_scale, SSM_LEARN_RATE, 0.0
    )
    return (
        layer_out[None],
        input_grad[None],
        attn_step,
        attn_moments_new,
        mlp_step,
        mlp_moments_new,
        norms_step,
        norm_moments_new,
        taps_step,
        tap_moments_new,
        ssm_step,
        ssm_moments_new,
    )


LANES = 128
RADIX = 8
HALF = 128


def transform_tables():
    rows = np.arange(HALF)
    length = RADIX * HALF
    waves = RADIX * rows[None, :, None] + np.arange(RADIX)[:, None, None] + 0.25
    angles = 2.0 * np.pi * np.mod(rows[None, None, :] * waves, length) / length
    cosines, sines = np.cos(angles), np.sin(angles)
    full = np.concatenate(
        [np.concatenate([cosines, sines], axis=2), np.concatenate([-sines, cosines], axis=2)], axis=1
    )


    def parts(matrix):
        matrix = matrix.astype(np.float32)
        high = matrix.astype(ml_dtypes.bfloat16)
        rest = (matrix - high.astype(np.float32)).astype(ml_dtypes.bfloat16)
        return np.stack([high, rest])

    return parts(full), parts(np.swapaxes(full, 1, 2))


def turned(value, angle):
    real, imaginary = value
    cosine, sine = math.cos(angle), math.sin(angle)
    if abs(sine) < 1e-12:
        return (real, imaginary) if cosine > 0 else (-real, -imaginary)
    if abs(cosine) < 1e-12:
        return (-imaginary, real) if sine > 0 else (imaginary, -real)
    return (real * cosine - imaginary * sine, real * sine + imaginary * cosine)


def small_transform(values, sign):
    count = len(values)
    if count == 1:
        return values
    even = small_transform(values[::2], sign)
    odd = small_transform(values[1::2], sign)
    low, high = [], []
    for index in range(count // 2):
        (er, ei), (tr, ti) = even[index], turned(odd[index], sign * 2.0 * math.pi * index / count)
        low.append((er + tr, ei + ti))
        high.append((er - tr, ei - ti))
    return low + high


def dot(left, right):
    return jnp.dot(left, right, preferred_element_type=jnp.float32)


def keep_parts(high_ref, low_ref, wave, row, cols, value):
    high = value.astype(jnp.bfloat16)
    high_ref[wave, pl.ds(row, 16), cols] = high
    if low_ref is not None:
        low_ref[wave, pl.ds(row, 16), cols] = (value - high.astype(jnp.float32)).astype(jnp.bfloat16)


def table_dot(table_high, table_low, high_ref, low_ref, wave):
    high = high_ref[wave]
    total = dot(table_high, high) + dot(table_low, high)
    return total if low_ref is None else total + dot(table_high, low_ref[wave])


def each_tile(width, rows, step, body):
    for block in range(width // LANES):

        def one(index, carry, block=block):
            body(pl.multiple_of(index * step, step), pl.ds(block * LANES, LANES))
            return carry

        lax.fori_loop(0, rows // step, one, 0)


def to_waves(width, read, used, w_ref, high_ref, low_ref, store):
    def first(row, cols):
        inputs = []
        for part in range(used):
            x = read(part * HALF, row, cols)
            angle = -2.0 * math.pi * part / 32.0
            inputs.append((x * math.cos(angle), x * math.sin(angle)) if part else (x, jnp.zeros_like(x)))
        while len(inputs) < RADIX:
            inputs.append((jnp.zeros_like(x), jnp.zeros_like(x)))
        for wave, value in enumerate(small_transform(inputs, -1.0)):
            for place, part in enumerate(value):
                keep_parts(high_ref, low_ref, wave, row + place * HALF, cols, part)

    each_tile(width, HALF, 16, first)

    def second(wave, carry):
        store(wave, table_dot(w_ref[0, wave], w_ref[1, wave], high_ref, low_ref, wave))
        return carry

    lax.fori_loop(0, RADIX, second, 0)


def product(width, left_ref, right_ref, conjugate, high_ref, low_ref):
    sign = -1.0 if conjugate else 1.0

    def one(wave, carry):
        def tile(row, cols):
            lr, li = left_ref[wave, pl.ds(row, 16), cols], left_ref[wave, pl.ds(row + HALF, 16), cols] * sign
            rr, ri = right_ref[wave, pl.ds(row, 16), cols], right_ref[wave, pl.ds(row + HALF, 16), cols]
            for place, part in enumerate((lr * rr - li * ri, lr * ri + li * rr)):
                keep_parts(high_ref, low_ref, wave, row + place * HALF, cols, part)

        each_tile(width, HALF, 16, tile)
        return carry

    lax.fori_loop(0, RADIX, one, 0)


def from_waves(width, w_ref, high_ref, low_ref, back_ref, put):
    def second(wave, carry):
        back_ref[wave] = table_dot(w_ref[0, wave], w_ref[1, wave], high_ref, low_ref, wave)
        return carry

    lax.fori_loop(0, RADIX, second, 0)
    scale = 1.0 / (RADIX * HALF)

    def first(row, cols):
        values = [
            (back_ref[wave, pl.ds(row, 16), cols], back_ref[wave, pl.ds(row + HALF, 16), cols])
            for wave in range(RADIX)
        ]
        for part, (real, imaginary) in enumerate(small_transform(values, 1.0)):
            angle = 2.0 * math.pi * part / 32.0
            put(part * HALF, row, cols, real * (math.cos(angle) * scale) - imaginary * (math.sin(angle) * scale))

    each_tile(width, HALF, 16, first)


def first_positions(width, count, w_ref, high_ref, low_ref):
    total = jnp.zeros((count, width), jnp.float32)
    for wave in range(RADIX):
        total = total + table_dot(w_ref[0, wave, :count, :], w_ref[1, wave, :count, :], high_ref, low_ref, wave)
    return total * (1.0 / (RADIX * HALF))


FINE = 32


def decay_sums(width, length, ssm_ref, out_ref):
    modes = ssm_ref.shape[1]
    steps = length // FINE
    out_ref[...] = jnp.zeros(out_ref.shape, jnp.float32)
    for block in range(width // LANES):
        cols = pl.ds(block * LANES, LANES)
        offsets = lax.broadcasted_iota(jnp.int32, (FINE, LANES), 0).astype(jnp.float32)

        def group(index, carry, cols=cols, offsets=offsets):
            base = pl.multiple_of(index * 8, 8)
            rates = jnp.exp(ssm_ref[0, pl.ds(base, 8), cols])
            leaps = jnp.exp(-rates * FINE)
            weights = ssm_ref[1, pl.ds(base, 8), cols]
            terms = tuple(weights[i : i + 1] * jnp.exp(-rates[i : i + 1] * offsets) for i in range(8))
            leap_rows = [jnp.broadcast_to(leaps[i : i + 1], (FINE, LANES)) for i in range(8)]

            def step(number, terms, leap_rows=leap_rows):
                rows = pl.ds(pl.multiple_of(number * FINE, FINE), FINE)
                total = out_ref[rows, cols]
                for term in terms:
                    total = total + term
                out_ref[rows, cols] = total
                return tuple(term * leap for term, leap in zip(terms, leap_rows))

            lax.fori_loop(0, steps, step, terms, unroll=4)
            return carry

        lax.fori_loop(0, modes // 8, group, 0)


def decay_gradients(block, length, ssm_ref, grad_ref, out_ref):
    modes = ssm_ref.shape[1]
    steps = length // FINE
    cols = pl.ds(block * LANES, LANES)
    offsets = lax.broadcasted_iota(jnp.int32, (FINE, LANES), 0).astype(jnp.float32)

    def group(index, carry):
        base = pl.multiple_of(index * 8, 8)
        rates = jnp.exp(ssm_ref[0, pl.ds(base, 8), cols])
        leaps = jnp.exp(-rates * FINE)
        plain_rows, slope_rows = [], []
        for modes_now in ((0, 1, 2, 3), (4, 5, 6, 7)):
            zero = offsets * 0.0
            leap_rows = [jnp.broadcast_to(leaps[i : i + 1], (FINE, LANES)) for i in modes_now]

            def step(number, sums, leap_rows=leap_rows):
                rows = grad_ref[pl.ds(pl.multiple_of((steps - 1 - number) * FINE, FINE), FINE), cols]
                return tuple((v * leap + rows, w * leap + v) for (v, w), leap in zip(sums, leap_rows))

            sums = lax.fori_loop(0, steps, step, tuple((zero, zero) for _ in modes_now), unroll=8)
            for i, (v, w) in zip(modes_now, sums):
                fine = jnp.exp(-rates[i : i + 1] * offsets)
                plain = fine * v
                slope = fine * w * (leaps[i : i + 1] * FINE) + plain * offsets
                plain_rows.append(jnp.sum(plain, axis=0, keepdims=True))
                slope_rows.append(jnp.sum(slope, axis=0, keepdims=True))
        out_ref[modes // 8 + index, :, cols] = jnp.concatenate(plain_rows, axis=0)
        out_ref[index, :, cols] = (
            -ssm_ref[1, pl.ds(base, 8), cols] * rates * jnp.concatenate(slope_rows, axis=0)
        )
        return carry

    lax.fori_loop(0, modes // 8, group, 0)


def layer_norm_parts(values):
    average = jnp.mean(values, axis=-1, keepdims=True)
    centred = values - average
    variance = jnp.mean(centred * centred, axis=-1, keepdims=True)
    inverse = lax.rsqrt(variance + EPS_NORM)
    return centred * inverse, inverse


def layer_norm_back(upstream, normal, inverse, gain_row):
    weighted = upstream * gain_row
    average = jnp.mean(weighted, axis=-1, keepdims=True)
    overlap = jnp.mean(weighted * normal, axis=-1, keepdims=True)
    into = (weighted - average - normal * overlap) * inverse
    return into, jnp.sum(upstream * normal, axis=0, keepdims=True), jnp.sum(upstream, axis=0, keepdims=True)


MESH = pl.DeviceIdType.MESH
TWO, FOUR = 2, 4
TAP_ROWS = 64
VMEM_LIMIT = 62 * 1024 * 1024


class Place:
    def __init__(self):
        self.s, self.d = lax.axis_index("seq"), lax.axis_index("dp")
        self.z, self.y, self.c = self.d // 4, (self.d // 2) % 2, self.d % 2

    def over_x(self):
        return (1 - self.s, self.d)

    def over_y(self):
        return (self.s, self.d + 2 - 4 * self.y)

    def over_core(self):
        return (self.s, self.d + 1 - 2 * self.c)

    def along_z(self, step):
        return (self.s, (self.d + 4 * step) % 16)

    def owner(self, index):
        return (self.s, index)


def send(source, target, send_sem, recv_sem, device):
    return pltpu.make_async_remote_copy(
        src_ref=source, dst_ref=target, send_sem=send_sem, recv_sem=recv_sem, device_id=device, device_id_type=MESH
    )


def greet_all(place):
    barrier = pltpu.get_barrier_semaphore()
    pl.semaphore_signal(barrier, inc=1, device_id=place.over_x(), device_id_type=MESH)

    def greet(step, carry):
        pl.semaphore_signal(
            barrier, inc=1, device_id=place.owner((place.d + step) % 16), device_id_type=MESH
        )
        return carry

    lax.fori_loop(1, 16, greet, 0)
    pl.semaphore_wait(barrier, 16)


WEIGHTS = (
    ("up", 0, 1536, "halved"),
    ("up", 1536, 1536, "halved"),
    ("out", 0, 768, "whole"),
    ("down", 0, 1536, "whole"),
    ("down", 1536, 1536, "whole"),
)


def forward_body(
    token_ref, qkv_ref, out_shard, mlp_shard, small_ref, ssm_ref, to_ref, from_ref,
    qkv_full, out_full, up_full, down_full, small_t, normed_ref, proj_ref, rows_ref,
    conv_ref, shifted_ref, kernel_w, taps_w, keys_w, mixed_w,
    token_all, small_all, gated_ref, line_ref, high_ref, low_ref, back_ref,
    own_sem, z_s, z_r, y_s, y_r, x_s, x_r, core_s, core_r, small_s, small_r, side_s, side_r,
):
    length, width = conv_ref.shape
    own_rows = token_ref.shape[0]
    place = Place()
    qkv = len(WEIGHTS)
    shards = {"up": mlp_shard.at[0], "down": mlp_shard.at[1], "out": out_shard}
    fulls = {"up": up_full, "down": down_full, "out": out_full}

    def columns(k):
        source, start, count, way = WEIGHTS[k]
        if way == "whole":
            return source, pl.ds(start, count)
        return source, pl.ds(pl.multiple_of(start + place.s * (count // 2), LANES), count // 2)

    def z_copy(k, step):
        if k == qkv:
            source, target = qkv_ref, qkv_full.at[place.z, place.y, place.c]
        else:
            name, cols = columns(k)
            source, target = shards[name].at[:, cols], fulls[name].at[place.z, place.y, place.c, :, cols]
        return send(source, target, z_s.at[k, step - 1], z_r.at[k, step - 1], place.along_z(step))

    def y_copy(k):
        if k == qkv:
            blocks = qkv_full.at[:, place.y, place.c]
        else:
            name, cols = columns(k)
            blocks = fulls[name].at[:, place.y, place.c, :, cols]
        return send(blocks, blocks, y_s.at[k], y_r.at[k], place.over_y())

    def x_copy(k):
        name, cols = columns(k)
        blocks = fulls[name].at[:, :, place.c, :, cols]
        return send(blocks, blocks, x_s.at[k], x_r.at[k], place.over_x())

    def core_copy(k):
        if k == qkv:
            blocks = qkv_full.at[:, :, place.c]
        else:
            name, start, count, _ = WEIGHTS[k]
            blocks = fulls[name].at[:, :, place.c, :, pl.ds(start, count)]
        return send(blocks, blocks, core_s.at[k], core_r.at[k], place.over_core())

    def own_copies():
        copies = []
        for k in range(qkv):
            name, cols = columns(k)
            target = fulls[name].at[place.z, place.y, place.c, :, cols]
            copies.append(pltpu.make_async_copy(shards[name].at[:, cols], target, own_sem.at[k]))
        return copies

    def start_z(k):
        for step in range(1, 4):
            z_copy(k, step).start()

    def z_to_y(k):
        for step in range(1, 4):
            z_copy(k, step).wait_recv()
        y_copy(k).start()

    def y_on(k):
        y_copy(k).wait_recv()
        if k != qkv and WEIGHTS[k][3] == "halved":
            x_copy(k).start()
        else:
            core_copy(k).start()

    def x_on(k):
        x_copy(k).wait_recv()
        core_copy(k).start()

    def small_copy(step):
        other = (place.d + step) % 16
        return send(small_ref, small_all.at[place.d], small_s.at[other], small_r.at[place.d], place.owner(other))

    def small_arrival(step):
        other = (place.d + step) % 16
        return send(small_ref, small_all.at[other], small_s.at[other], small_r.at[other], place.owner(other))

    def over_peers(action):
        def one(step, carry):
            action(step)
            return carry

        lax.fori_loop(1, 16, one, 0)

    token_copy = send(token_ref, token_all.at[place.s], side_s.at[0], side_r.at[0], place.over_x())
    gated_copy = send(
        gated_ref.at[1 - place.s], rows_ref.at[place.s], side_s.at[1], side_r.at[1], place.over_x()
    )

    greet_all(place)
    over_peers(lambda step: small_copy(step).start())
    start_z(qkv)
    token_copy.start()
    for copy in own_copies():
        copy.start()
    qkv_full[place.z, place.y, place.c] = qkv_ref[...]
    small_all[place.d] = small_ref[...]

    def keep(target):
        def store(wave, value):
            target[wave] = value

        return store

    def lines(base, row, cols):
        return line_ref[pl.ds(base + row, 16), cols]

    def column(index, cols):
        return pl.ds(index * width + cols.start, cols.size)

    decay_sums(width, length, ssm_ref, line_ref)
    z_to_y(qkv)
    for k in range(qkv):
        if k < 2:
            start_z(k)
    to_waves(width, lines, RADIX, to_ref, high_ref, low_ref, keep(kernel_w))
    over_peers(lambda step: small_arrival(step).wait_recv())
    small_t[...] = small_all[...].reshape(16 * small_all.shape[1], LANES).astype(jnp.float32).T
    taps_cols = pl.multiple_of(place.s * width, LANES)

    def read_taps(base, row, cols):
        taps = small_t[pl.ds(base + row, 16), pl.ds(pl.multiple_of(taps_cols + cols.start, LANES), LANES)]
        inside = lax.broadcasted_iota(jnp.int32, taps.shape, 0) + (base + row) < TAP_ROWS
        return jnp.where(inside, taps, 0.0)

    y_on(qkv)
    to_waves(width, read_taps, 1, to_ref, high_ref, low_ref, keep(taps_w))

    def normalize(source, begin):
        def one(index, carry):
            row = pl.multiple_of(index * 32, 32)
            normal, _ = layer_norm_parts(source[pl.ds(row, 32), :].astype(jnp.float32))
            scaled = normal * small_t[TAP_ROWS : TAP_ROWS + 1, :] + small_t[TAP_ROWS + 1 : TAP_ROWS + 2, :]
            normed_ref[pl.ds(pl.multiple_of(begin + row, 32), 32), :] = scaled.astype(jnp.bfloat16)
            return carry

        lax.fori_loop(0, own_rows // 32, one, 0)

    def project(begin):
        weight = qkv_full[...].reshape(normed_ref.shape[1], 3 * width)

        def one(index, carry):
            row = pl.ds(pl.multiple_of(begin + index * 256, 256), 256)
            proj_ref[row, :] = dot(normed_ref[row, :], weight)
            return carry

        lax.fori_loop(0, own_rows // 256, one, 0)

    own_begin, other_begin = place.s * own_rows, (1 - place.s) * own_rows
    normalize(token_ref, own_begin)
    for copy in own_copies():
        copy.wait()
    z_to_y(0)
    start_z(2)
    token_copy.wait_recv()
    normalize(token_all.at[1 - place.s], other_begin)
    core_copy(qkv).wait_recv()
    project(own_begin)
    z_to_y(1)
    y_on(0)
    start_z(3)
    project(other_begin)
    z_to_y(2)
    start_z(4)
    y_on(1)
    to_waves(
        width, lambda base, row, cols: proj_ref[pl.ds(base + row, 16), column(1, cols)],
        RADIX, to_ref, high_ref, low_ref, keep(keys_w),
    )
    product(width, taps_w, keys_w, False, high_ref, low_ref)
    y_on(2)
    x_on(0)

    def put_shifted(base, row, cols, value):
        rows = pl.ds(base + row, 16)
        shifted_ref[rows, cols] = value
        mixed = value * proj_ref[rows, column(2, cols)]
        line_ref[rows, cols] = mixed.astype(jnp.bfloat16).astype(jnp.float32)

    from_waves(width, from_ref, high_ref, low_ref, back_ref, put_shifted)
    z_to_y(3)
    to_waves(width, lines, RADIX, to_ref, high_ref, low_ref, keep(mixed_w))
    x_on(1)
    product(width, kernel_w, mixed_w, False, high_ref, low_ref)

    def put_conv(base, row, cols, value):
        rows = pl.ds(base + row, 16)
        rounded = value.astype(jnp.bfloat16)
        conv_ref[rows, cols] = rounded
        gated = (proj_ref[rows, cols] * rounded.astype(jnp.float32)).astype(jnp.bfloat16)
        gated_ref[base // own_rows, pl.ds(base % own_rows + row, 16), cols] = gated

    from_waves(width, from_ref, high_ref, low_ref, back_ref, put_conv)
    gated_copy.start()
    z_to_y(4)
    y_on(3)
    rows_ref[place.s] = gated_ref[place.s]
    y_on(4)
    gated_copy.wait_recv()
    for k in range(qkv):
        core_copy(k).wait_recv()

    over_peers(lambda step: small_copy(step).wait_send())
    token_copy.wait_send()
    gated_copy.wait_send()
    for k in range(qkv + 1):
        for step in range(1, 4):
            z_copy(k, step).wait_send()
        y_copy(k).wait_send()
        core_copy(k).wait_send()
        if k != qkv and WEIGHTS[k][3] == "halved":
            x_copy(k).wait_send()


def forward_mixer(tokens, qkv_shard, out_shard, mlp_shard, small, ssm, to_table, from_table):
    own_rows, model = tokens.shape
    owned = qkv_shard.shape[0]
    width = qkv_shard.shape[1] // 3
    length = 2 * own_rows
    hidden = mlp_shard.shape[2]
    f32, low = jnp.float32, jnp.bfloat16
    waves = (RADIX, 2 * HALF, width)
    vmem, anywhere = pl.BlockSpec(memory_space=pltpu.VMEM), pl.BlockSpec(memory_space=pl.ANY)
    shape = jax.ShapeDtypeStruct
    owners = (FOUR, TWO, TWO, owned)
    count = len(WEIGHTS)
    dma = pltpu.SemaphoreType.DMA
    return pl.pallas_call(
        forward_body,
        out_shape=(
            shape(owners + (3 * width,), low),
            shape(owners + (model,), low),
            shape(owners + (hidden,), low),
            shape(owners + (hidden,), low),
            shape((LANES, model), f32),
            shape((length, model), low),
            shape((length, 3 * width), f32),
            shape((2, own_rows, width), low),
            shape((length, width), low),
            shape((length, width), f32),
        )
        + (shape(waves, f32),) * 4,
        in_specs=[vmem, vmem, anywhere, anywhere, vmem, vmem, vmem, vmem],
        out_specs=(vmem, anywhere, anywhere, anywhere) + (vmem,) * 10,
        scratch_shapes=[
            pltpu.VMEM((2, own_rows, model), low),
            pltpu.VMEM((16,) + small.shape, low),
            pltpu.VMEM((2, own_rows, width), low),
            pltpu.VMEM((length, width), f32),
            pltpu.VMEM(waves, low),
            pltpu.VMEM(waves, low),
            pltpu.VMEM(waves, f32),
            dma((count,)),
            dma((count + 1, 3)),
            dma((count + 1, 3)),
            dma((count + 1,)),
            dma((count + 1,)),
            dma((count + 1,)),
            dma((count + 1,)),
            dma((count + 1,)),
            dma((count + 1,)),
            dma((16,)),
            dma((16,)),
            dma((2,)),
            dma((2,)),
        ],
        compiler_params=pltpu.CompilerParams(collective_id=2, has_side_effects=True, vmem_limit_bytes=VMEM_LIMIT),
        name="forward_mixer",
    )(tokens, qkv_shard, out_shard, mlp_shard, small, ssm, to_table, from_table)


PIECES = (
    ("down", 0, 1536, "whole"),
    ("up", 1536, 1536, "halved"),
    ("down", 1536, 1536, "whole"),
    ("out", 0, 768, "halved"),
    ("up", 0, 1536, "whole"),
    ("qkv", 0, 1152, "apart"),
)
QKV = len(PIECES) - 1


def add_blocks(put, sources, count):
    def one(index, carry):
        total = sources[0](index).astype(jnp.float32)
        for source in sources[1:]:
            total = total + source(index).astype(jnp.float32)
        put(index, total)
        return carry

    lax.fori_loop(0, count, one, 0)


def piece_halves(k):
    return TWO if PIECES[k][3] == "halved" else 1


def backward_body(*refs):
    count = len(PIECES)
    (
        gated_grad_ref, proj_ref, conv_ref, shifted_ref, kernel_w, taps_w, keys_w, mixed_w, ssm_ref, to_ref, from_ref,
        normed_ref, qkv_ref, token_ref, residual_ref, small_t, norm_two_ref, down_ref, up_ref, out_ref,
    ), refs = refs[:20], refs[20:]
    outs, refs = refs[:count], refs[count:]
    (small_out, ssm_out, input_out), refs = refs[:3], refs[3:]
    near, refs = refs[:count], refs[count:]
    from_x = dict(zip([k for k in range(count) if piece_halves(k) == TWO], refs))
    refs = refs[len(from_x):]
    from_y, from_z, final, last = (refs[i * count : (i + 1) * count] for i in range(4))
    refs = refs[4 * count :]
    (
        own_ref, grad_all, query_ref, value_ref, spectrum, line_ref, decay_ref, wave_ref, high_ref, back_ref,
        grad_proj, qkv_grad, gn_send, gn_own, gn_last, small_rows, small_ref, small_all, small_sum, small_last,
        ssm_ref_all, ssm_all, ssm_sum,
    ), refs = refs[:23], refs[23:]
    (
        load_sem, own_sem, core_s, core_r, x_s, x_r, y_s, y_r, z_s, z_r, f_s, f_r, sm_s, sm_r, ss_s, ss_r, sg_s, sg_r,
        side_s, side_r,
    ) = refs
    length, width = conv_ref.shape
    own_rows = token_ref.shape[0]
    place = Place()
    grads = {"down": down_ref, "up": up_ref, "out": out_ref, "qkv": qkv_grad}

    def core_copy(k, h):
        source, start, columns, _ = PIECES[k]
        part = columns // piece_halves(k)
        blocks = grads[source].at[:, :, 1 - place.c, :, pl.ds(start + h * part, part)]
        return send(blocks, near[k].at[h], core_s.at[k, h], core_r.at[k, h], place.over_core())

    def own_copy(k, h):
        source, start, columns, _ = PIECES[k]
        part = columns // piece_halves(k)
        blocks = grads[source].at[:, :, place.c, :, pl.ds(start + h * part, part)]
        return pltpu.make_async_copy(blocks, own_ref.at[k % 2, :, :, :, pl.ds(h * part, part)], own_sem.at[k % 2, h])

    def x_copy(k):
        return send(near[k].at[1 - place.s], from_x[k], x_s.at[k], x_r.at[k], place.over_x())

    def kept(k):
        return near[k].at[place.s] if piece_halves(k) == TWO else near[k].at[0]

    def y_copy(k):
        return send(kept(k).at[:, 1 - place.y], from_y[k], y_s.at[k], y_r.at[k], place.over_y())

    def z_copy(k, step):
        other = (place.z + step) % 4
        return send(
            kept(k).at[other, place.y], from_z[k].at[step - 1], z_s.at[k, step - 1], z_r.at[k, step - 1],
            place.along_z(step),
        )

    def last_copy(k):
        return send(final[k], last[k], f_s.at[k], f_r.at[k], place.over_x())

    def load_own(k):
        for h in range(piece_halves(k)):
            own_copy(k, h).start()

    def add_core(k):
        part = PIECES[k][2] // piece_halves(k)
        for h in range(piece_halves(k)):
            core_copy(k, h).wait_recv()
            if k != QKV:
                own_copy(k, h).wait()

            def own(i, h=h):
                if k == QKV:
                    return qkv_grad[i // 2, i % 2, place.c]
                return own_ref[k % 2, i // 2, i % 2, :, h * part : (h + 1) * part]

            def put(i, total, h=h):
                near[k][h, i // 2, i % 2] = total.astype(jnp.bfloat16)

            add_blocks(put, [own, lambda i, h=h: near[k][h, i // 2, i % 2]], 8)
        if piece_halves(k) == TWO:
            x_copy(k).start()
        else:
            y_copy(k).start()

    def add_x(k):
        x_copy(k).wait_recv()

        def put(i, total):
            kept(k)[i // 2, i % 2] = total.astype(jnp.bfloat16)

        add_blocks(put, [lambda i: kept(k)[i // 2, i % 2], lambda i: from_x[k][i // 2, i % 2]], 8)
        y_copy(k).start()

    def add_y(k):
        y_copy(k).wait_recv()

        def put(i, total):
            kept(k)[i, place.y] = total.astype(jnp.bfloat16)

        add_blocks(put, [lambda i: kept(k)[i, place.y], lambda i: from_y[k][i]], 4)
        for step in range(1, 4):
            z_copy(k, step).start()

    def add_z(k):
        for step in range(1, 4):
            z_copy(k, step).wait_recv()
        total = kept(k)[place.z, place.y].astype(jnp.float32)
        for step in range(3):
            total = total + from_z[k][step].astype(jnp.float32)
        final[k][...] = total.astype(jnp.bfloat16)
        last_copy(k).start()

    def finish(k):
        last_copy(k).wait_recv()
        if PIECES[k][3] == "whole":
            outs[k][...] = final[k][...].astype(jnp.float32) + last[k][...].astype(jnp.float32)
        else:
            outs[k][place.s] = final[k][...]
            outs[k][1 - place.s] = last[k][...]

    def over_peers(action):
        def one(step, carry):
            action(step)
            return carry

        lax.fori_loop(1, 16, one, 0)

    def to_peer(source, target, send_sem, recv_sem, step):
        other = (place.d + step) % 16
        return send(source.at[other], target.at[place.d], send_sem.at[other], recv_sem.at[place.d], place.owner(other))

    def from_peer(target, send_sem, recv_sem, step):
        other = (place.d + step) % 16
        return send(target.at[other], target.at[other], send_sem.at[other], recv_sem.at[other], place.owner(other))

    def share(step):
        other = (place.d + step) % 16
        return send(ssm_sum.at[place.d], ssm_sum.at[place.d], sg_s.at[other], sg_r.at[place.d], place.owner(other))

    grad_copy = send(
        gated_grad_ref.at[:, pl.ds(pl.multiple_of((1 - place.s) * width, LANES), width)], grad_all.at[place.s],
        side_s.at[0], side_r.at[0], place.over_x(),
    )
    gn_copy = send(gn_send, gn_last, side_s.at[1], side_r.at[1], place.over_x())
    small_copy = send(small_sum, small_last, side_s.at[2], side_r.at[2], place.over_x())
    spectra = (kernel_w, mixed_w, taps_w, keys_w)

    def load_spectrum(i):
        return pltpu.make_async_copy(spectra[i], spectrum.at[i % 2], load_sem.at[i % 2])

    query_copy = pltpu.make_async_copy(proj_ref.at[:, pl.ds(0, width)], query_ref, load_sem.at[2])
    value_copy = pltpu.make_async_copy(proj_ref.at[:, pl.ds(2 * width, width)], value_ref, load_sem.at[3])

    greet_all(place)
    grad_copy.start()
    for k in range(QKV):
        for h in range(piece_halves(k)):
            core_copy(k, h).start()
    load_own(0)
    load_own(1)
    query_copy.start()
    value_copy.start()
    load_spectrum(0).start()
    load_spectrum(1).start()
    grad_all[place.s] = gated_grad_ref[:, pl.ds(pl.multiple_of(place.s * width, LANES), width)]
    for k in range(QKV):
        add_core(k)
        if k + 2 < QKV:
            load_own(k + 2)

    def keep(wave, value):
        wave_ref[wave] = value

    def lines(base, row, cols):
        return line_ref[pl.ds(base + row, 16), cols]

    def column(index, cols):
        return pl.ds(index * width + cols.start, cols.size)

    def read_conv_grad(base, row, cols):
        rows = pl.ds(base + row, 16)
        gradient = grad_all[base // own_rows, pl.ds(base % own_rows + row, 16), cols].astype(jnp.float32)
        grad_proj[rows, cols] = (gradient * conv_ref[rows, cols].astype(jnp.float32)).astype(jnp.bfloat16)
        return (gradient * query_ref[rows, cols]).astype(jnp.bfloat16).astype(jnp.float32)

    query_copy.wait()
    value_copy.wait()
    grad_copy.wait_recv()
    to_waves(width, read_conv_grad, RADIX, to_ref, high_ref, None, keep)
    add_y(0)
    load_spectrum(0).wait()
    product(width, spectrum.at[0], wave_ref, True, high_ref, None)
    load_spectrum(2).start()

    def put_mixed(base, row, cols, value):
        rows = pl.ds(base + row, 16)
        gradient = value.astype(jnp.bfloat16).astype(jnp.float32)
        grad_proj[rows, column(2, cols)] = (gradient * shifted_ref[rows, cols]).astype(jnp.bfloat16)
        line_ref[rows, cols] = gradient * value_ref[rows, cols]

    from_waves(width, from_ref, high_ref, None, back_ref, put_mixed)
    add_x(1)
    load_spectrum(1).wait()
    product(width, spectrum.at[1], wave_ref, True, high_ref, None)
    load_spectrum(3).start()

    def put_kernel(base, row, cols, value):
        decay_ref[pl.ds(base + row, 16), cols] = value

    from_waves(width, from_ref, high_ref, None, back_ref, put_kernel)
    add_y(2)
    to_waves(width, lines, RADIX, to_ref, high_ref, None, keep)
    add_z(0)
    load_spectrum(2).wait()
    product(width, spectrum.at[0], wave_ref, True, high_ref, None)

    def put_keys(base, row, cols, value):
        grad_proj[pl.ds(base + row, 16), column(1, cols)] = value.astype(jnp.bfloat16)

    from_waves(width, from_ref, high_ref, None, back_ref, put_keys)
    add_x(3)

    def project_back(begin, put):
        def one(index, carry):
            row = pl.multiple_of(index * 256, 256)
            value = lax.dot_general(
                grad_proj[pl.ds(pl.multiple_of(begin + row, 256), 256), :], qkv_ref[...], (((1,), (1,)), ((), ())),
                preferred_element_type=jnp.float32,
            )
            put(pl.ds(row, 256), value)
            return carry

        lax.fori_loop(0, own_rows // 256, one, 0)

    def put_send(rows, value):
        gn_send[rows, :] = value.astype(jnp.bfloat16)

    def put_own(rows, value):
        gn_own[rows, :] = value

    project_back((1 - place.s) * own_rows, put_send)
    gn_copy.start()
    for pair in range(TWO):
        columns = 2 * 4 * qkv_grad.shape[3]
        value = lax.dot_general(
            normed_ref[:, pair * columns : (pair + 1) * columns], grad_proj[...], (((0,), (0,)), ((), ())),
            preferred_element_type=jnp.float32,
        )
        qkv_grad[2 * pair : 2 * pair + 2] = value.astype(jnp.bfloat16).reshape((2,) + qkv_grad.shape[1:])
    core_copy(QKV, 0).start()
    add_y(4)
    project_back(place.s * own_rows, put_own)
    add_core(QKV)
    add_y(1)
    load_spectrum(3).wait()
    product(width, spectrum.at[1], wave_ref, True, high_ref, None)
    small_rows[...] = jnp.zeros(small_rows.shape, jnp.float32)
    small_rows[:TAP_ROWS, pl.ds(pl.multiple_of(place.s * width, LANES), width)] = first_positions(
        width, TAP_ROWS, from_ref, high_ref, None
    )
    add_z(2)
    add_y(3)
    decay_gradients(0, length, ssm_ref, decay_ref, ssm_ref_all)
    add_y(QKV)
    add_z(4)
    decay_gradients(1, length, ssm_ref, decay_ref, ssm_ref_all)
    add_z(1)
    add_z(3)
    decay_gradients(2, length, ssm_ref, decay_ref, ssm_ref_all)
    over_peers(lambda step: to_peer(ssm_ref_all, ssm_all, ss_s, ss_r, step).start())
    gn_copy.wait_recv()

    def norm_back(index, sums):
        rows = pl.ds(pl.multiple_of(index * 32, 32), 32)
        normal, inverse = layer_norm_parts(token_ref[rows, :].astype(jnp.float32))
        upstream = gn_own[rows, :] + gn_last[rows, :].astype(jnp.float32)
        into, gain, bias = layer_norm_back(upstream, normal, inverse, small_t[TAP_ROWS : TAP_ROWS + 1, :])
        input_out[rows, :] = residual_ref[rows, :] + into
        return sums[0] + gain, sums[1] + bias

    zero = jnp.sum(norm_two_ref[...], axis=0, keepdims=True) * 0.0
    gain, bias = lax.fori_loop(0, own_rows // 32, norm_back, (zero, zero))
    small_rows[TAP_ROWS : TAP_ROWS + 1, :] = gain
    small_rows[TAP_ROWS + 1 : TAP_ROWS + 2, :] = bias
    small_rows[TAP_ROWS + 2 : TAP_ROWS + 4, :] = norm_two_ref[...]
    small_ref[...] = small_rows[...].T.astype(jnp.bfloat16).reshape(small_ref.shape)
    over_peers(lambda step: to_peer(small_ref, small_all, sm_s, sm_r, step).start())
    add_z(QKV)

    over_peers(lambda step: from_peer(ssm_all, ss_s, ss_r, step).wait_recv())
    ssm_all[place.d] = ssm_ref_all[place.d]
    total = ssm_all[0]
    for index in range(1, 16):
        total = total + ssm_all[index]
    ssm_sum[place.d] = total
    over_peers(lambda step: share(step).start())
    over_peers(lambda step: from_peer(small_all, sm_s, sm_r, step).wait_recv())

    def add_small(step, total):
        return total + small_all[(place.d + step) % 16].astype(jnp.float32)

    small_sum[...] = lax.fori_loop(1, 16, add_small, small_ref[place.d].astype(jnp.float32)).astype(jnp.bfloat16)
    small_copy.start()
    for k in range(count):
        finish(k)
    over_peers(lambda step: from_peer(ssm_sum, sg_s, sg_r, step).wait_recv())
    ssm_out[...] = ssm_sum[...]
    small_copy.wait_recv()
    small_out[...] = small_sum[...].astype(jnp.float32) + small_last[...].astype(jnp.float32)

    for k in range(count):
        for h in range(piece_halves(k)):
            core_copy(k, h).wait_send()
        if piece_halves(k) == TWO:
            x_copy(k).wait_send()
        y_copy(k).wait_send()
        for step in range(1, 4):
            z_copy(k, step).wait_send()
        last_copy(k).wait_send()
    for copy in (grad_copy, gn_copy, small_copy):
        copy.wait_send()
    over_peers(lambda step: to_peer(small_ref, small_all, sm_s, sm_r, step).wait_send())
    over_peers(lambda step: to_peer(ssm_ref_all, ssm_all, ss_s, ss_r, step).wait_send())
    over_peers(lambda step: share(step).wait_send())


def backward_mixer(
    gated_grad, proj, conv, shifted, kernel_w, taps_w, keys_w, mixed_w, ssm, to_table, from_table, normed, qkv, tokens,
    residual, small, norm_two, down, up, out,
):
    f32, low = jnp.float32, jnp.bfloat16
    count = len(PIECES)
    length, width = conv.shape
    own_rows, model = tokens.shape
    owned = down.shape[3]
    waves = (RADIX, 2 * HALF, width)
    vmem, anywhere = pl.BlockSpec(memory_space=pltpu.VMEM), pl.BlockSpec(memory_space=pl.ANY)
    results, near, from_x, from_y, from_z, final, last = [], [], [], [], [], [], []
    for k, (_, _, columns, way) in enumerate(PIECES):
        halves = piece_halves(k)
        part = columns // halves
        whole = way == "whole"
        results.append(jax.ShapeDtypeStruct((owned, part) if whole else (TWO, owned, part), f32 if whole else low))
        near.append(pltpu.VMEM((halves, FOUR, TWO, owned, part), low))
        if halves == TWO:
            from_x.append(pltpu.VMEM((FOUR, TWO, owned, part), low))
        from_y.append(pltpu.VMEM((FOUR, owned, part), low))
        from_z.append(pltpu.VMEM((3, owned, part), low))
        final.append(pltpu.VMEM((owned, part), low))
        last.append(pltpu.VMEM((owned, part), low))
    dma = pltpu.SemaphoreType.DMA
    slots = (16, 8, width)
    packed = (16, owned, LANES)
    results += [
        jax.ShapeDtypeStruct(packed[1:], f32),
        jax.ShapeDtypeStruct(slots, f32),
        jax.ShapeDtypeStruct((own_rows, model), f32),
    ]
    return pl.pallas_call(
        backward_body,
        out_shape=tuple(results),
        in_specs=[vmem, anywhere, vmem, vmem] + [anywhere] * 4 + [vmem] * 9 + [anywhere] * 3,
        out_specs=(vmem,) * len(results),
        scratch_shapes=near
        + from_x
        + from_y
        + from_z
        + final
        + last
        + [
            pltpu.VMEM((2, FOUR, TWO, owned, 1536), low),
            pltpu.VMEM((2, own_rows, width), low),
            pltpu.VMEM((length, width), f32),
            pltpu.VMEM((length, width), f32),
            pltpu.VMEM((2,) + waves, f32),
            pltpu.VMEM((length, width), f32),
            pltpu.VMEM((length, width), f32),
            pltpu.VMEM(waves, f32),
            pltpu.VMEM(waves, low),
            pltpu.VMEM(waves, f32),
            pltpu.VMEM((length, 3 * width), low),
            pltpu.VMEM((FOUR, TWO, TWO, owned, 3 * width), low),
            pltpu.VMEM((own_rows, model), low),
            pltpu.VMEM((own_rows, model), f32),
            pltpu.VMEM((own_rows, model), low),
            pltpu.VMEM((LANES, model), f32),
            pltpu.VMEM(packed, low),
            pltpu.VMEM(packed, low),
            pltpu.VMEM(packed[1:], low),
            pltpu.VMEM(packed[1:], low),
            pltpu.VMEM(slots, f32),
            pltpu.VMEM(slots, f32),
            pltpu.VMEM(slots, f32),
            dma((4,)),
            dma((2, TWO)),
            dma((count, TWO)),
            dma((count, TWO)),
        ]
        + [dma((count,))] * 4
        + [dma((count, 3))] * 2
        + [dma((count,))] * 2
        + [dma((16,))] * 6
        + [dma((3,))] * 2,
        compiler_params=pltpu.CompilerParams(collective_id=1, has_side_effects=True, vmem_limit_bytes=VMEM_LIMIT),
        name="backward_mixer",
    )(
        gated_grad, proj, conv, shifted, kernel_w, taps_w, keys_w, mixed_w, ssm, to_table, from_table, normed, qkv, tokens,
        residual, small, norm_two, down, up, out,
    )


def per_device_split(
    tokens,
    cotangent,
    attn_weight,
    mlp_weight,
    norms,
    taps,
    ssm_params,
    attn_moments,
    mlp_moments,
    norm_moments,
    tap_moments,
    ssm_moments,
):
    f32, low = jnp.float32, jnp.bfloat16
    rows, width = tokens.shape[1:]
    shares = lax.axis_size("seq")
    owners = lax.axis_size("dp")
    length = rows * shares
    part = width // shares
    half = lax.axis_index("seq")
    tap_count = taps.shape[0]
    to_table, from_table = map(jnp.asarray, transform_tables())

    owned = attn_weight.shape[0]
    columns = lax.dynamic_index_in_dim(attn_weight.reshape(owned, 4, shares, part), half, 2, False)
    qkv_shard = columns[:, :3].reshape(owned, 3 * part)
    small = jnp.concatenate([taps, norms, jnp.zeros((LANES - 4 - tap_count, owned), low)]).T
    ssm_turned = jnp.swapaxes(ssm_params, 1, 2)
    (
        qkv_full, out_full, up_full, down_full, small_full, normed_low, proj, gated_parts,
        conv, shifted, kernel_w, taps_w, keys_w, mixed_w,
    ) = forward_mixer(
        tokens[0], qkv_shard, attn_weight[:, 3 * width :], mlp_weight, small, ssm_turned, to_table, from_table
    )
    qkv_full = qkv_full.reshape(width, 3 * part)
    out_full = out_full.reshape(width, width)
    mlp_full = (up_full.reshape(width, -1), down_full.reshape(width, -1))
    norm_rows = small_full[tap_count : tap_count + 4]
    gated_rows = jnp.concatenate([gated_parts[0], gated_parts[1]], axis=1)
    inputs = tokens[0].astype(f32)
    residual = inputs + dot(gated_rows, out_full)
    normal_two, inverse_two = layer_norm_parts(residual)
    normed_two = (normal_two * norm_rows[2] + norm_rows[3]).astype(low)
    before = dot(normed_two, mlp_full[0])
    active, gelu_pull = jax.vjp(jax.nn.gelu, before)
    active_low = active.astype(low)
    grad_after = cotangent[0]
    layer_out = (
        residual + jnp.einsum("tf,df->td", active_low, mlp_full[1], preferred_element_type=f32)
    ).astype(low)
    grad_active = dot(grad_after, mlp_full[1])
    grad_down = jnp.einsum("td,tf->df", grad_after, active_low, preferred_element_type=f32)
    grad_before = gelu_pull(grad_active)[0].astype(low)
    grad_up = jnp.einsum("td,tf->df", normed_two, grad_before, preferred_element_type=f32)
    grad_normed_two = jnp.einsum("tf,df->td", grad_before, mlp_full[0], preferred_element_type=f32)
    into_two, gain_two, bias_two = layer_norm_back(grad_normed_two, normal_two, inverse_two, norm_rows[2])
    grad_residual = grad_after.astype(f32) + into_two
    grad_branch = grad_residual.astype(low)
    grad_out = jnp.einsum("td,te->de", gated_rows, grad_branch, preferred_element_type=f32)
    grad_gated = jnp.einsum("te,de->td", grad_branch, out_full, preferred_element_type=f32).astype(low)

    def by_owner(gradient):
        return gradient.astype(low).reshape(FOUR, TWO, TWO, owned, gradient.shape[1])

    scale = 1.0 / math.sqrt(owners * length)
    sums = backward_mixer(
        grad_gated, proj, conv, shifted, kernel_w, taps_w, keys_w, mixed_w, ssm_turned, to_table, from_table,
        normed_low, qkv_full, tokens[0], grad_residual, small_full, jnp.concatenate([gain_two, bias_two]),
        by_owner(grad_down), by_owner(grad_up), by_owner(grad_out),
    )
    down_sum = jnp.concatenate([sums[0], sums[2]], axis=1)
    up_sum = jnp.concatenate([sums[4], sums[1][0].astype(f32), sums[1][1].astype(f32)], axis=1)
    qkv_sum = jnp.swapaxes(sums[5].reshape(shares, owned, 3, part), 0, 1).swapaxes(1, 2)
    attn_sum = jnp.concatenate([qkv_sum.reshape(owned, 3 * width), sums[3][0], sums[3][1]], axis=1)
    mlp_sum = jnp.stack([up_sum, down_sum])
    small_sum = sums[6].T
    small_sum = jnp.concatenate([small_sum[tap_count : tap_count + 4], small_sum[:tap_count]])
    ssm_sum = jnp.swapaxes(sums[7].reshape(ssm_turned.shape), 1, 2)
    input_grad = sums[8]

    attn_step, attn_new = adam_update(
        attn_weight.astype(f32), attn_moments, attn_sum.astype(f32) * scale, LEARN_RATE, DECAY_RATE
    )
    mlp_step, mlp_new = adam_update(
        mlp_weight.astype(f32), mlp_moments, mlp_sum.astype(f32) * scale, LEARN_RATE, DECAY_RATE
    )
    norms_step, norm_new = adam_update(norms.astype(f32), norm_moments, small_sum[:4] * scale, LEARN_RATE, 0.0)
    taps_step, tap_new = adam_update(taps.astype(f32), tap_moments, small_sum[4:] * scale, LEARN_RATE, DECAY_RATE)
    ssm_step, ssm_new = adam_update(ssm_params, ssm_moments, ssm_sum * scale, SSM_LEARN_RATE, 0.0)
    return (
        layer_out[None],
        input_grad[None],
        attn_step,
        attn_new,
        mlp_step,
        mlp_new,
        norms_step,
        norm_new,
        taps_step,
        tap_new,
        ssm_step,
        ssm_new,
    )


def solution(mesh):
    fits = (mesh.shape["seq"], mesh.shape["dp"]) == (2, 16)

    def chosen(tokens, cotangent, attn_weight, mlp_weight, norms, taps, *others):
        fast = fits and tokens.shape[1:] == (RADIX * HALF // 2, 6 * LANES) and taps.shape[0] == TAP_ROWS
        plan = per_device_split if fast else per_device
        return plan(tokens, cotangent, attn_weight, mlp_weight, norms, taps, *others)

    return jax.shard_map(
        chosen,
        mesh=mesh,
        in_specs=(
            P("dp", "seq", None),
            P("dp", "seq", None),
            P("dp", None),
            P(None, "dp", None),
            P(None, "dp"),
            P(None, "dp"),
            P(None, "seq", None),
            P(None, "dp", None),
            P(None, None, "dp", None),
            P(None, None, "dp"),
            P(None, None, "dp"),
            P(None, None, "seq", None),
        ),
        out_specs=(
            P("dp", "seq", None),
            P("dp", "seq", None),
            P("dp", None),
            P(None, "dp", None),
            P(None, "dp", None),
            P(None, None, "dp", None),
            P(None, "dp"),
            P(None, None, "dp"),
            P(None, "dp"),
            P(None, None, "dp"),
            P(None, "seq", None),
            P(None, None, "seq", None),
        ),
        check_vma=False,
    )
```

profile of v0, /device:TPU:0, one launch (start us, length us, event | category | flops | bytes accessed | tf_op | source)
XLA Modules:
  0.0 270.2 jit_solution(4258800075533336540)
XLA Ops:
  0.7 1.2 reshape.276
  4.4 104.4 %forward_mixer.1 = (bf16[4,2,2,48,1152]{4,3,2,1,0:T(8,128)(2,1)}, bf16[4,2,2,48,768]{4,3,2,1,0:T(8,128)(2,1)}, bf16[4,2,2,48,3072]{4,3,2,1,0:T(8,128)(2,1)}, bf1...) custom-call(bf16[512,768]{1,0:T(8,128)(2,1)} %bitcast.154, ...), custom_call_target="tpu_custom_call" | custom-call | tf_op jit(solution)/shard_map/forward_mixer/pallas_call | solution.py:863
  108.9 1.3 slice_bitcast_fusion.1
  110.2 2.3 fusion.48
  112.5 0.8 slice_reduce_fusion.1
  113.7 2.8 %fusion.45 = f32[512,3072]{1,0:T(8,128)S(1)} fusion(bf16[768,3072]{1,0:T(8,128)(2,1)S(1)} %bitcast.168, f32[512,768]{1,0:T(8,128)S(1)} %get-tuple-element.155, f32[768]{0:T(1024)S(1)} %get-tuple-element.123, f32[768]{0:T(1024)S(1)} %get-tuple-element.122, f32[512]{0:T(512)S(1)} %add_rsqrt_fusion, f32[512]{0:T(512)S(1)} %broadcast_multiply_fusion.5), kind=kOutput, calls=%fused_computation.120 | convolution fusion | flops 2417885184 | bytes 12593152 | tf_op jit(solution)/shard_map/dot_general | solution.py:397
  116.5 4.9 %fusion.10 = bf16[1,512,768]{2,1,0:T(8,128)(2,1)} fusion(f32[512,768]{1,0:T(8,128)S(1)} %get-tuple-element.155, bf16[768,3072]{1,0:T(8,128)(2,1)S(1)} %bitcast.172, f32[512,3072]{1,0:T(8,128)S(1)} %fusion.45), kind=kOutput, calls=%fused_computation.29 | convolution fusion | flops 2430861312 | bytes 13369344 | tf_op jit(solution)/shard_map/tf,df->td/dot_general | solution.py:1392
  121.4 6.2 %fusion.6 = bf16[512,3072]{1,0:T(8,128)(2,1)S(1)} fusion(f32[512,3072]{1,0:T(8,128)S(1)} %fusion.45, bf16[768,3072]{1,0:T(8,128)(2,1)S(1)} %bitcast.173, bf16[1,512,768]{2,1,0:T(8,128)(2,1)S(1)} %copy-done.8), kind=kOutput, calls=%fused_computation.8 | convolution fusion | flops 2447376384 | bytes 14942208 | tf_op jit(solution)/shard_map/dot_general | solution.py:397
  127.6 3.1 %multiply_reduce_fusion = (f32[768]{0:T(1024)S(1)}, f32[512]{0:T(512)S(1)}, f32[512]{0:T(512)S(1)}, f32[768]{0:T(1024)S(1)}, f32[512,768]{1,0:T(8,128)S(1)}) fusion(f32[512,768]{1,0:T(8,128)S(1)} %get-tuple-element.155, f32[512]{0:T(512)S(1)} %add_rsqrt_fusion, f32[512]{0:T(512)S(1)} %broadcast_multiply_fusion.5, f32[768]{0:T(1024)S(1)} %get-tuple-element.122, ...), kind=kOutput, calls=%fused_computation.18 | convolution fusion | flops 2419455488 | bytes 11027456 | tf_op jit(solution)/shard_map/tf,df->td/dot_general | solution.py:1398
  132.0 1.7 convolution_convert_fusion.3.refs_0_
  134.3 4.8 %convolution_convert_fusion.1 = bf16[3072,768]{0,1:T(8,128)(2,1)} fusion(bf16[1,512,768]{2,1,0:T(8,128)(2,1)S(1)} %copy-done.8, f32[512,3072]{1,0:T(8,128)S(1)} %fusion.45), kind=kOutput, calls=%fused_computation.16 | convolution fusion | flops 2432434176 | bytes 11796480 | tf_op jit(solution)/shard_map/td,tf->df/dot_general | solution.py:1395
  139.0 4.9 %convolution_convert_fusion = bf16[768,3072]{1,0:T(8,128)(2,1)} fusion(bf16[512,3072]{1,0:T(8,128)(2,1)S(1)} %fusion.6, f32[512,768]{1,0:T(8,128)S(1)} %get-tuple-element.155, f32[768]{0:T(1024)S(1)} %get-tuple-element.123, f32[768]{0:T(1024)S(1)} %get-tuple-element.122, f32[512]{0:T(512)S(1)} %add_rsqrt_fusion, f32[512]{0:T(512)S(1)} %broadcast_multiply_fusion.5), kind=kOutput, calls=%fused_computation.15 | convolution fusion | flops 2420244480 | bytes 9447424 | tf_op jit(solution)/shard_map/td,tf->df/dot_general | solution.py:1397
  143.9 1.8 convolution_convert_fusion.2
  145.7 107.4 %backward_mixer.1 = (f32[48,1536]{1,0:T(8,128)}, bf16[2,48,768]{2,1,0:T(8,128)(2,1)}, f32[48,1536]{1,0:T(8,128)}, bf16[2,48,384]{2,1,0:T(8,128)(2,1)}, f32[48,15...) custom-call(bf16[512,768]{1,0:T(8,128)(2,1)} %convolution_convert_fu, ...), custom_call_target="tpu_custom_call" | custom-call | tf_op jit(solution)/shard_map/backward_mixer/pallas_call | solution.py:1290
  253.2 0.9 fusion.46
  254.1 1.0 reshape.285
  255.5 1.3 fusion.24
  257.2 1.1 pad_maximum_fusion.1
  258.9 1.1 copy-done
  260.1 1.9 fusion.16
  262.6 1.6 pad_maximum_fusion
  267.5 0.8 fusion.37
  268.3 0.8 pad_maximum_fusion.8
  269.1 1.1 copy.99
  (90 shorter events, 10.0 us)
Async XLA Ops:
  0.6 2.3 copy-start.7
  0.7 2.9 %copy-start.19 = (bf16[4,48]{1,0:T(4,128)(2,1)S(1)}, bf16[4,48]{1,0:T(4,128)(2,1)}, u32[]{:S(2)}) copy-start(bf16[4,48]{1,0:T(4,128)(2,1)} %param.18) | copy-start | bytes 1156
  0.7 3.1 %copy-start.16 = (bf16[64,48]{0,1:T(8,128)(2,1)S(1)}, bf16[64,48]{0,1:T(8,128)(2,1)}, u32[]{:S(2)}) copy-start(bf16[64,48]{0,1:T(8,128)(2,1)} %param.19) | copy-start | bytes 18436
  108.9 1.4 copy-start.3
  110.2 3.5 %copy-start.20 = (bf16[4,2,2,48,3072]{4,3,2,1,0:T(8,128)(2,1)S(1)}, bf16[4,2,2,48,3072]{4,3,2,1,0:T(8,128)(2,1)}, u32[]{:S(2)}) copy-start(bf16[4,2,2,48,3072]{4,3,2,1,0:T(8,128)(2,1)} %get-tuple-element.38) | copy-start | bytes 14155780
  113.4 3.1 %slice-start = ((s8[4718592]{0:T(1024)(128)(4,1)}), s8[4194304]{0:T(1024)(128)(4,1)S(1)}, s32[]{:S(2)}) async-start(s8[4718592]{0:T(1024)(128)(4,1)} %bitcast.170), calls=%async_computation | async-start | bytes 8388608
  113.7 2.8 %slice-start.1 = ((s8[4718592]{0:T(1024)(128)(4,1)}), s8[524288]{0:T(1024)(128)(4,1)S(1)}, s32[]{:S(2)}) async-start(s8[4718592]{0:T(1024)(128)(4,1)} %bitcast.170), calls=%async_computation.1 | async-start | bytes 1048576
  116.5 4.9 %copy-start.8 = (bf16[1,512,768]{2,1,0:T(8,128)(2,1)S(1)}, bf16[1,512,768]{2,1,0:T(8,128)(2,1)}, u32[]{:S(2)}) copy-start(bf16[1,512,768]{2,1,0:T(8,128)(2,1)} %param.15) | copy-start | bytes 2359300
  130.7 1.3 copy-start.21
  132.0 11.9 %copy-start.1 = (f32[512,768]{1,0:T(8,128)}, f32[512,768]{1,0:T(8,128)S(1)}, u32[]{:S(2)}) copy-start(f32[512,768]{1,0:T(8,128)S(1)} %multiply_add_fusion.refs_14_) | copy-start | bytes 4718596
  253.2 2.3 copy-start.2
  257.2 1.1 copy-start.12
  257.2 1.2 copy-start.11
  257.2 1.3 copy-start.14
  257.2 1.6 copy-start.10
  258.3 1.7 copy-start
  258.3 1.8 copy-start.4
  262.6 1.6 copy-start.18
  262.6 1.8 copy-start.15
  262.6 3.6 %copy-start.17 = (f32[2,64,48]{1,2,0:T(8,128)S(1)}, f32[2,64,48]{1,2,0:T(8,128)}, u32[]{:S(2)}) copy-start(f32[2,64,48]{1,2,0:T(8,128)} %param.24) | copy-start | bytes 73732
  262.6 4.8 %copy-start.13 = (f32[16,8,384]{2,1,0:T(8,128)S(1)}, f32[16,8,384]{2,1,0:T(8,128)}, u32[]{:S(2)}) copy-start(f32[16,8,384]{2,1,0:T(8,128)} %get-tuple-element.57) | copy-start | bytes 589828
  262.6 4.9 %copy-start.5 = (f32[2,384,64]{1,2,0:T(8,128)S(1)}, f32[2,384,64]{1,2,0:T(8,128)}, u32[]{:S(2)}) copy-start(f32[2,384,64]{1,2,0:T(8,128)} %param.20) | copy-start | bytes 589828
  264.2 3.3 %copy-start.9 = (f32[2,2,384,64]{2,3,1,0:T(8,128)S(1)}, f32[2,2,384,64]{2,3,1,0:T(8,128)}, u32[]{:S(2)}) copy-start(f32[2,2,384,64]{2,3,1,0:T(8,128)} %param.25) | copy-start | bytes 1179652
  266.8 2.3 copy-start.6
where the time goes:
time: 271 us; the launch traced here: 270 us
  Pallas kernels  212 us (78%)
  matrix products  32.3 us (12%)
  other arithmetic  12.6 us (5%)
  local copies, waits for them, and re-layouts  12.5 us (5%)
    pallas_call x1, Pallas kernels, backward_mixer(): pl.pallas_call(backward_body, out_shape=tuple(results), in_specs=[vmem, a...  107 us
    pallas_call x1, Pallas kernels, forward_mixer(): pl.pallas_call(forward_body, out_shape=(shape(owners + (3 * width,), low)...  104 us
    dot_general x3, matrix products, dot(): return jnp.dot(left, right, preferred_element_type=jnp.float32)  11.3 us
    another operation x8, other arithmetic, adam_update(): return (step_size, jnp.stack([first_new, second_new]))  6.23 us

commit v1 on v0

--- a/solution.py
+++ b/solution.py
@@ -617,26 +617,44 @@
 
 
 WEIGHTS = (
+    ("out", 0, 768, "whole"),
     ("up", 0, 1536, "halved"),
+    ("down", 0, 1536, "whole"),
     ("up", 1536, 1536, "halved"),
-    ("out", 0, 768, "whole"),
-    ("down", 0, 1536, "whole"),
     ("down", 1536, 1536, "whole"),
 )
+OUT_W, UP_FIRST, DOWN_FIRST, UP_LAST, DOWN_LAST, QKV_W = range(len(WEIGHTS) + 1)
+HIDDEN_BLOCK = 768
+
+
+def dot_right(left, right):
+    return lax.dot_general(left, right, (((1,), (1,)), ((), ())), preferred_element_type=jnp.float32)
+
+
+def dot_left(left, right):
+    return lax.dot_general(left, right, (((0,), (0,)), ((), ())), preferred_element_type=jnp.float32)
+
+
+def gelu_parts(x):
+    slope = math.sqrt(2.0 / math.pi)
+    square = x * x
+    bent = jnp.tanh(slope * x * (1.0 + 0.044715 * square))
+    upper = 0.5 + 0.5 * bent
+    return x * upper, upper + 0.5 * x * (1.0 - bent * bent) * (slope * (1.0 + 3.0 * 0.044715 * square))
 
 
 def forward_body(
-    token_ref, qkv_ref, out_shard, mlp_shard, small_ref, ssm_ref, to_ref, from_ref,
-    qkv_full, out_full, up_full, down_full, small_t, normed_ref, proj_ref, rows_ref,
-    conv_ref, shifted_ref, kernel_w, taps_w, keys_w, mixed_w,
-    token_all, small_all, gated_ref, line_ref, high_ref, low_ref, back_ref,
-    own_sem, z_s, z_r, y_s, y_r, x_s, x_r, core_s, core_r, small_s, small_r, side_s, side_r,
+    token_ref, cotangent_ref, attn_shard, mlp_shard, small_ref, ssm_ref, to_ref, from_ref,
+    qkv_full, up_full, down_full, small_t, normed_ref, query_out, value_out, conv_ref, shifted_ref,
+    kernel_out, taps_out, keys_out, mixed_out, layer_out, residual_grad, norm_two_out, gated_grad, up_grad, down_grad, out_grad,
+    qkv_ref, token_all, small_all, gated_ref, rows_ref, out_full, grad_send,
+    own_sem, z_s, z_r, y_s, y_r, x_s, x_r, core_s, core_r, small_s, small_r, side_s, side_r, store_sem, load_sem,
 ):
     length, width = conv_ref.shape
-    own_rows = token_ref.shape[0]
+    own_rows, model = token_ref.shape
     place = Place()
-    qkv = len(WEIGHTS)
-    shards = {"up": mlp_shard.at[0], "down": mlp_shard.at[1], "out": out_shard}
+    f32, low = jnp.float32, jnp.bfloat16
+    shards = {"up": mlp_shard.at[0], "down": mlp_shard.at[1], "out": attn_shard.at[:, pl.ds(3 * model, model)]}
     fulls = {"up": up_full, "down": down_full, "out": out_full}
 
     def columns(k):
@@ -646,7 +664,7 @@
         return source, pl.ds(pl.multiple_of(start + place.s * (count // 2), LANES), count // 2)
 
     def z_copy(k, step):
-        if k == qkv:
+        if k == QKV_W:
             source, target = qkv_ref, qkv_full.at[place.z, place.y, place.c]
         else:
             name, cols = columns(k)
@@ -654,7 +672,7 @@
         return send(source, target, z_s.at[k, step - 1], z_r.at[k, step - 1], place.along_z(step))
 
     def y_copy(k):
-        if k == qkv:
+        if k == QKV_W:
             blocks = qkv_full.at[:, place.y, place.c]
         else:
             name, cols = columns(k)
@@ -667,7 +685,7 @@
         return send(blocks, blocks, x_s.at[k], x_r.at[k], place.over_x())
 
     def core_copy(k):
-        if k == qkv:
+        if k == QKV_W:
             blocks = qkv_full.at[:, :, place.c]
         else:
             name, start, count, _ = WEIGHTS[k]
@@ -676,7 +694,7 @@
 
     def own_copies():
         copies = []
-        for k in range(qkv):
+        for k in range(QKV_W):
             name, cols = columns(k)
             target = fulls[name].at[place.z, place.y, place.c, :, cols]
             copies.append(pltpu.make_async_copy(shards[name].at[:, cols], target, own_sem.at[k]))
@@ -686,29 +704,9 @@
         for step in range(1, 4):
             z_copy(k, step).start()
 
-    def z_to_y(k):
+    def wait_z(k):
         for step in range(1, 4):
             z_copy(k, step).wait_recv()
-        y_copy(k).start()
-
-    def y_on(k):
-        y_copy(k).wait_recv()
-        if k != qkv and WEIGHTS[k][3] == "halved":
-            x_copy(k).start()
-        else:
-            core_copy(k).start()
-
-    def x_on(k):
-        x_copy(k).wait_recv()
-        core_copy(k).start()
-
-    def small_copy(step):
-        other = (place.d + step) % 16
-        return send(small_ref, small_all.at[place.d], small_s.at[other], small_r.at[place.d], place.owner(other))
-
-    def small_arrival(step):
-        other = (place.d + step) % 16
-        return send(small_ref, small_all.at[other], small_s.at[other], small_r.at[other], place.owner(other))
 
     def over_peers(action):
         def one(step, carry):
@@ -717,140 +715,360 @@
 
         lax.fori_loop(1, 16, one, 0)
 
+    def small_copy(step):
+        other = (place.d + step) % 16
+        return send(small_ref, small_all.at[place.d], small_s.at[other], small_r.at[place.d], place.owner(other))
+
+    def small_arrival(step):
+        other = (place.d + step) % 16
+        return send(small_ref, small_all.at[other], small_s.at[other], small_r.at[other], place.owner(other))
+
     token_copy = send(token_ref, token_all.at[place.s], side_s.at[0], side_r.at[0], place.over_x())
-    gated_copy = send(
-        gated_ref.at[1 - place.s], rows_ref.at[place.s], side_s.at[1], side_r.at[1], place.over_x()
-    )
-
+    gated_copy = send(gated_ref.at[1 - place.s], rows_ref.at[place.s], side_s.at[1], side_r.at[1], place.over_x())
+    grad_copy = send(grad_send, gated_grad.at[place.s], side_s.at[2], side_r.at[2], place.over_x())
+
+    def step_one():
+        wait_z(QKV_W)
+        y_copy(QKV_W).start()
+        start_z(OUT_W)
+        for copy in own_copies():
+            copy.wait()
+
+    def step_two():
+        wait_z(OUT_W)
+        start_z(UP_FIRST)
+
+    def step_three():
+        y_copy(QKV_W).wait_recv()
+        core_copy(QKV_W).start()
+        y_copy(OUT_W).start()
+
+    def step_four():
+        wait_z(UP_FIRST)
+        start_z(DOWN_FIRST)
+
+    def step_five():
+        y_copy(OUT_W).wait_recv()
+        core_copy(OUT_W).start()
+        y_copy(UP_FIRST).start()
+
+    def step_six():
+        y_copy(UP_FIRST).wait_recv()
+        x_copy(UP_FIRST).start()
+
+    def step_seven():
+        wait_z(DOWN_FIRST)
+        y_copy(DOWN_FIRST).start()
+        start_z(UP_LAST)
+
+    def step_eight():
+        wait_z(UP_LAST)
+        start_z(DOWN_LAST)
+
+    def step_nine():
+        x_copy(UP_FIRST).wait_recv()
+        core_copy(UP_FIRST).start()
+
+    def step_ten():
+        y_copy(DOWN_FIRST).wait_recv()
+        core_copy(DOWN_FIRST).start()
+        y_copy(UP_LAST).start()
+
+    def step_eleven():
+        y_copy(UP_LAST).wait_recv()
+        x_copy(UP_LAST).start()
+
+    def step_twelve():
+        wait_z(DOWN_LAST)
+        y_copy(DOWN_LAST).start()
+
+    def step_thirteen():
+        x_copy(UP_LAST).wait_recv()
+        core_copy(UP_LAST).start()
+
+    def step_fourteen():
+        y_copy(DOWN_LAST).wait_recv()
+        core_copy(DOWN_LAST).start()
+
+    for j in range(3):
+        cols = pl.ds(pl.multiple_of((2 * j + place.s) * width, LANES), width)
+        qkv_ref[:, j * width : (j + 1) * width] = attn_shard[:, cols]
     greet_all(place)
+    start_z(QKV_W)
     over_peers(lambda step: small_copy(step).start())
-    start_z(qkv)
     token_copy.start()
     for copy in own_copies():
         copy.start()
     qkv_full[place.z, place.y, place.c] = qkv_ref[...]
     small_all[place.d] = small_ref[...]
 
-    def keep(target):
-        def store(wave, value):
-            target[wave] = value
-
-        return store
-
-    def lines(base, row, cols):
-        return line_ref[pl.ds(base + row, 16), cols]
-
-    def column(index, cols):
-        return pl.ds(index * width + cols.start, cols.size)
-
-    decay_sums(width, length, ssm_ref, line_ref)
-    z_to_y(qkv)
-    for k in range(qkv):
-        if k < 2:
-            start_z(k)
-    to_waves(width, lines, RADIX, to_ref, high_ref, low_ref, keep(kernel_w))
-    over_peers(lambda step: small_arrival(step).wait_recv())
-    small_t[...] = small_all[...].reshape(16 * small_all.shape[1], LANES).astype(jnp.float32).T
-    taps_cols = pl.multiple_of(place.s * width, LANES)
-
-    def read_taps(base, row, cols):
-        taps = small_t[pl.ds(base + row, 16), pl.ds(pl.multiple_of(taps_cols + cols.start, LANES), LANES)]
-        inside = lax.broadcasted_iota(jnp.int32, taps.shape, 0) + (base + row) < TAP_ROWS
-        return jnp.where(inside, taps, 0.0)
-
-    y_on(qkv)
-    to_waves(width, read_taps, 1, to_ref, high_ref, low_ref, keep(taps_w))
-
-    def normalize(source, begin):
-        def one(index, carry):
-            row = pl.multiple_of(index * 32, 32)
-            normal, _ = layer_norm_parts(source[pl.ds(row, 32), :].astype(jnp.float32))
-            scaled = normal * small_t[TAP_ROWS : TAP_ROWS + 1, :] + small_t[TAP_ROWS + 1 : TAP_ROWS + 2, :]
-            normed_ref[pl.ds(pl.multiple_of(begin + row, 32), 32), :] = scaled.astype(jnp.bfloat16)
+    def mixer(line_ref, high_ref, low_ref, back_ref, proj_ref, kernel_w, other_w, keys_w):
+        def keep(target):
+            def store(wave, value):
+                target[wave] = value
+
+            return store
+
+        def lines(base, row, cols):
+            return line_ref[pl.ds(base + row, 16), cols]
+
+        def column(index, cols):
+            return pl.ds(index * width + cols.start, cols.size)
+
+        stores = [
+            pltpu.make_async_copy(kernel_w, kernel_out, store_sem.at[0]),
+            pltpu.make_async_copy(other_w, taps_out, store_sem.at[1]),
+            pltpu.make_async_copy(keys_w, keys_out, store_sem.at[2]),
+            pltpu.make_async_copy(other_w, mixed_out, store_sem.at[3]),
+            pltpu.make_async_copy(proj_ref.at[:, pl.ds(0, width)], query_out, store_sem.at[4]),
+            pltpu.make_async_copy(proj_ref.at[:, pl.ds(2 * width, width)], value_out, store_sem.at[5]),
+        ]
+        decay_sums(width, length, ssm_ref, line_ref)
+        step_one()
+        to_waves(width, lines, RADIX, to_ref, high_ref, low_ref, keep(kernel_w))
+        stores[0].start()
+        over_peers(lambda step: small_arrival(step).wait_recv())
+        small_t[...] = small_all[...].reshape(16 * small_all.shape[1], LANES).astype(f32).T
+        taps_cols = pl.multiple_of(place.s * width, LANES)
+
+        def read_taps(base, row, cols):
+            taps = small_t[pl.ds(base + row, 16), pl.ds(pl.multiple_of(taps_cols + cols.start, LANES), LANES)]
+            inside = lax.broadcasted_iota(jnp.int32, taps.shape, 0) + (base + row) < TAP_ROWS
+            return jnp.where(inside, taps, 0.0)
+
+        def normalize(source, begin):
+            def one(index, carry):
+                row = pl.multiple_of(index * 32, 32)
+                normal, _ = layer_norm_parts(source[pl.ds(row, 32), :].astype(f32))
+                scaled = normal * small_t[TAP_ROWS : TAP_ROWS + 1, :] + small_t[TAP_ROWS + 1 : TAP_ROWS + 2, :]
+                normed_ref[pl.ds(pl.multiple_of(begin + row, 32), 32), :] = scaled.astype(low)
+                return carry
+
+            lax.fori_loop(0, own_rows // 32, one, 0)
+
+        def project(begin):
+            weight = qkv_full[...].reshape(model, 3 * width)
+
+            def one(index, carry):
+                row = pl.ds(pl.multiple_of(begin + index * 256, 256), 256)
+                proj_ref[row, :] = dot(normed_ref[row, :], weight)
+                return carry
+
+            lax.fori_loop(0, own_rows // 256, one, 0)
+
+        own_begin, other_begin = place.s * own_rows, (1 - place.s) * own_rows
+        normalize(token_ref, own_begin)
+        step_two()
+        token_copy.wait_recv()
+        normalize(token_all.at[1 - place.s], other_begin)
+        step_three()
+        to_waves(width, read_taps, 1, to_ref, high_ref, low_ref, keep(other_w))
+        stores[1].start()
+        step_four()
+        core_copy(QKV_W).wait_recv()
+        project(own_begin)
+        project(other_begin)
+        stores[4].start()
+        stores[5].start()
+        step_five()
+        to_waves(
+            width, lambda base, row, cols: proj_ref[pl.ds(base + row, 16), column(1, cols)],
+            RADIX, to_ref, high_ref, low_ref, keep(keys_w),
+        )
+        stores[2].start()
+        product(width, other_w, keys_w, False, high_ref, low_ref)
+        step_six()
+
+        def put_shifted(base, row, cols, value):
+            rows = pl.ds(base + row, 16)
+            shifted_ref[rows, cols] = value
+            mixed = value * proj_ref[rows, column(2, cols)]
+            line_ref[rows, cols] = mixed.astype(low).astype(f32)
+
+        from_waves(width, from_ref, high_ref, low_ref, back_ref, put_shifted)
+        step_seven()
+        stores[1].wait()
+        to_waves(width, lines, RADIX, to_ref, high_ref, low_ref, keep(other_w))
+        stores[3].start()
+        product(width, kernel_w, other_w, False, high_ref, low_ref)
+        step_eight()
+
+        def put_conv(base, row, cols, value):
+            rows = pl.ds(base + row, 16)
+            rounded = value.astype(low)
+            conv_ref[rows, cols] = rounded
+            gated = (proj_ref[rows, cols] * rounded.astype(f32)).astype(low)
+            gated_ref[base // own_rows, pl.ds(base % own_rows + row, 16), cols] = gated
+
+        from_waves(width, from_ref, high_ref, low_ref, back_ref, put_conv)
+        gated_copy.start()
+        for i in (0, 2, 3, 4, 5):
+            stores[i].wait()
+
+    waves = (RADIX, 2 * HALF, width)
+    pl.run_scoped(
+        mixer,
+        pltpu.VMEM((length, width), f32),
+        pltpu.VMEM(waves, low),
+        pltpu.VMEM(waves, low),
+        pltpu.VMEM(waves, f32),
+        pltpu.VMEM((length, 3 * width), f32),
+        pltpu.VMEM(waves, f32),
+        pltpu.VMEM(waves, f32),
+        pltpu.VMEM(waves, f32),
+    )
+    rows_ref[place.s] = gated_ref[place.s]
+
+    def feed_forward(
+        up_w, down_w, up_g, down_g, residual_ref, normed_two, normed_turned, cot_turned, active_ref, before_ref,
+        out_sum, normed_grad,
+    ):
+        block_shape = up_g.shape
+        blocks = up_full.shape[4] // HIDDEN_BLOCK
+
+        def load(j):
+            cols = pl.ds(j * HIDDEN_BLOCK, HIDDEN_BLOCK)
+            return [
+                pltpu.make_async_copy(full.at[:, :, :, :, cols], held.at[j % 2], load_sem.at[i, j % 2])
+                for i, (full, held) in enumerate(((up_full, up_w), (down_full, down_w)))
+            ]
+
+        def store(j):
+            cols = pl.ds(j * HIDDEN_BLOCK, HIDDEN_BLOCK)
+            return [
+                pltpu.make_async_copy(held, full.at[:, :, :, :, cols], store_sem.at[i])
+                for i, (full, held) in enumerate(((up_grad, up_g), (down_grad, down_g)))
+            ]
+
+        step_nine()
+        cot_turned[...] = cotangent_ref[...].T
+        step_ten()
+        core_copy(OUT_W).wait_recv()
+        gated_copy.wait_recv()
+        out_w = out_full[...].reshape(model, model)
+
+        def branch(index, carry):
+            rows = pl.ds(pl.multiple_of(index * 256, 256), 256)
+            value = dot(rows_ref[0, rows, :], out_w[:width]) + dot(rows_ref[1, rows, :], out_w[width:])
+            residual_ref[rows, :] = token_ref[rows, :].astype(f32) + value
             return carry
 
-        lax.fori_loop(0, own_rows // 32, one, 0)
-
-    def project(begin):
-        weight = qkv_full[...].reshape(normed_ref.shape[1], 3 * width)
-
-        def one(index, carry):
-            row = pl.ds(pl.multiple_of(begin + index * 256, 256), 256)
-            proj_ref[row, :] = dot(normed_ref[row, :], weight)
+        lax.fori_loop(0, own_rows // 256, branch, 0)
+
+        def normalize(index, carry):
+            rows = pl.ds(pl.multiple_of(index * 32, 32), 32)
+            normal, _ = layer_norm_parts(residual_ref[rows, :])
+            scaled = normal * small_t[TAP_ROWS + 2 : TAP_ROWS + 3, :] + small_t[TAP_ROWS + 3 : TAP_ROWS + 4, :]
+            normed_two[rows, :] = scaled.astype(low)
             return carry
 
-        lax.fori_loop(0, own_rows // 256, one, 0)
-
-    own_begin, other_begin = place.s * own_rows, (1 - place.s) * own_rows
-    normalize(token_ref, own_begin)
-    for copy in own_copies():
-        copy.wait()
-    z_to_y(0)
-    start_z(2)
-    token_copy.wait_recv()
-    normalize(token_all.at[1 - place.s], other_begin)
-    core_copy(qkv).wait_recv()
-    project(own_begin)
-    z_to_y(1)
-    y_on(0)
-    start_z(3)
-    project(other_begin)
-    z_to_y(2)
-    start_z(4)
-    y_on(1)
-    to_waves(
-        width, lambda base, row, cols: proj_ref[pl.ds(base + row, 16), column(1, cols)],
-        RADIX, to_ref, high_ref, low_ref, keep(keys_w),
-    )
-    product(width, taps_w, keys_w, False, high_ref, low_ref)
-    y_on(2)
-    x_on(0)
-
-    def put_shifted(base, row, cols, value):
-        rows = pl.ds(base + row, 16)
-        shifted_ref[rows, cols] = value
-        mixed = value * proj_ref[rows, column(2, cols)]
-        line_ref[rows, cols] = mixed.astype(jnp.bfloat16).astype(jnp.float32)
-
-    from_waves(width, from_ref, high_ref, low_ref, back_ref, put_shifted)
-    z_to_y(3)
-    to_waves(width, lines, RADIX, to_ref, high_ref, low_ref, keep(mixed_w))
-    x_on(1)
-    product(width, kernel_w, mixed_w, False, high_ref, low_ref)
-
-    def put_conv(base, row, cols, value):
-        rows = pl.ds(base + row, 16)
-        rounded = value.astype(jnp.bfloat16)
-        conv_ref[rows, cols] = rounded
-        gated = (proj_ref[rows, cols] * rounded.astype(jnp.float32)).astype(jnp.bfloat16)
-        gated_ref[base // own_rows, pl.ds(base % own_rows + row, 16), cols] = gated
-
-    from_waves(width, from_ref, high_ref, low_ref, back_ref, put_conv)
-    gated_copy.start()
-    z_to_y(4)
-    y_on(3)
-    rows_ref[place.s] = gated_ref[place.s]
-    y_on(4)
-    gated_copy.wait_recv()
-    for k in range(qkv):
-        core_copy(k).wait_recv()
+        lax.fori_loop(0, own_rows // 32, normalize, 0)
+        core_copy(UP_FIRST).wait_recv()
+        core_copy(DOWN_FIRST).wait_recv()
+        for copy in load(0) + load(1):
+            copy.start()
+        normed_turned[...] = normed_two[...].T
+        step_eleven()
+        step_twelve()
+        for j in range(blocks):
+            if j == blocks // 2:
+                step_thirteen()
+                step_fourteen()
+                core_copy(UP_LAST).wait_recv()
+                core_copy(DOWN_LAST).wait_recv()
+                for copy in load(j) + load(j + 1):
+                    copy.start()
+            for copy in load(j):
+                copy.wait()
+            up = up_w[j % 2].reshape(model, HIDDEN_BLOCK)
+            down = down_w[j % 2].reshape(model, HIDDEN_BLOCK)
+
+            def rows_of(index, carry, up=up, down=down, j=j):
+                rows = pl.ds(pl.multiple_of(index * 256, 256), 256)
+                active, slope = gelu_parts(dot(normed_two[rows, :], up))
+                active = active.astype(low)
+                active_ref[rows, :] = active
+                grad_before = (dot(cotangent_ref[rows, :], down) * slope).astype(low)
+                before_ref[rows, :] = grad_before
+                out_part = dot_right(active, down)
+                grad_part = dot_right(grad_before, up)
+                if j:
+                    out_part = out_part + out_sum[rows, :]
+                    grad_part = grad_part + normed_grad[rows, :]
+                out_sum[rows, :] = out_part
+                normed_grad[rows, :] = grad_part
+                return carry
+
+            lax.fori_loop(0, own_rows // 256, rows_of, 0)
+            if j:
+                for copy in store(j - 1):
+                    copy.wait()
+            down_g[...] = dot(cot_turned[...], active_ref[...]).astype(low).reshape(block_shape)
+            up_g[...] = dot(normed_turned[...], before_ref[...]).astype(low).reshape(block_shape)
+            for copy in store(j):
+                copy.start()
+
+        def norm_back(index, sums):
+            rows = pl.ds(pl.multiple_of(index * 32, 32), 32)
+            normal, inverse = layer_norm_parts(residual_ref[rows, :])
+            into, gain, bias = layer_norm_back(
+                normed_grad[rows, :], normal, inverse, small_t[TAP_ROWS + 2 : TAP_ROWS + 3, :]
+            )
+            total = cotangent_ref[rows, :].astype(f32) + into
+            residual_grad[rows, :] = total
+            active_ref[rows, :] = total.astype(low)
+            layer_out[rows, :] = (residual_ref[rows, :] + out_sum[rows, :]).astype(low)
+            return sums[0] + gain, sums[1] + bias
+
+        zero = small_t[TAP_ROWS : TAP_ROWS + 1, :] * 0.0
+        gain, bias = lax.fori_loop(0, own_rows // 32, norm_back, (zero, zero))
+        norm_two_out[0:1, :] = gain
+        norm_two_out[1:2, :] = bias
+        part_shape = (2,) + out_full.shape[1:]
+        other_w = out_full[pl.ds(2 * (1 - place.s), 2)].reshape(width, model)
+        grad_send[...] = dot_right(active_ref[...], other_w).astype(low)
+        grad_copy.start()
+        own_w = out_full[pl.ds(2 * place.s, 2)].reshape(width, model)
+        gated_grad[place.s] = dot_right(active_ref[...], own_w).astype(low)
+        for h in range(2):
+            out_grad[2 * h : 2 * h + 2] = dot_left(rows_ref[h], active_ref[...]).astype(low).reshape(part_shape)
+        for copy in store(blocks - 1):
+            copy.wait()
+        grad_copy.wait_recv()
+
+    block = (FOUR, TWO, TWO, out_full.shape[3], HIDDEN_BLOCK)
+    pl.run_scoped(
+        feed_forward,
+        pltpu.VMEM((2,) + block, low),
+        pltpu.VMEM((2,) + block, low),
+        pltpu.VMEM(block, low),
+        pltpu.VMEM(block, low),
+        pltpu.VMEM((own_rows, model), f32),
+        pltpu.VMEM((own_rows, model), low),
+        pltpu.VMEM((model, own_rows), low),
+        pltpu.VMEM((model, own_rows), low),
+        pltpu.VMEM((own_rows, HIDDEN_BLOCK), low),
+        pltpu.VMEM((own_rows, HIDDEN_BLOCK), low),
+        pltpu.VMEM((own_rows, model), f32),
+        pltpu.VMEM((own_rows, model), f32),
+    )
 
     over_peers(lambda step: small_copy(step).wait_send())
-    token_copy.wait_send()
-    gated_copy.wait_send()
-    for k in range(qkv + 1):
+    for copy in (token_copy, gated_copy, grad_copy):
+        copy.wait_send()
+    for k in range(QKV_W + 1):
         for step in range(1, 4):
             z_copy(k, step).wait_send()
         y_copy(k).wait_send()
         core_copy(k).wait_send()
-        if k != qkv and WEIGHTS[k][3] == "halved":
+        if k != QKV_W and WEIGHTS[k][3] == "halved":
             x_copy(k).wait_send()
 
 
-def forward_mixer(tokens, qkv_shard, out_shard, mlp_shard, small, ssm, to_table, from_table):
+def forward_layer(tokens, cotangent, attn_shard, mlp_shard, small, ssm, to_table, from_table):
     own_rows, model = tokens.shape
-    owned = qkv_shard.shape[0]
-    width = qkv_shard.shape[1] // 3
+    owned = attn_shard.shape[0]
+    width = model // 2
     length = 2 * own_rows
     hidden = mlp_shard.shape[2]
     f32, low = jnp.float32, jnp.bfloat16
@@ -858,50 +1076,62 @@
     vmem, anywhere = pl.BlockSpec(memory_space=pltpu.VMEM), pl.BlockSpec(memory_space=pl.ANY)
     shape = jax.ShapeDtypeStruct
     owners = (FOUR, TWO, TWO, owned)
-    count = len(WEIGHTS)
+    count = len(WEIGHTS) + 1
     dma = pltpu.SemaphoreType.DMA
+    outs = (
+        (shape(owners + (3 * width,), low), vmem),
+        (shape(owners + (hidden,), low), anywhere),
+        (shape(owners + (hidden,), low), anywhere),
+        (shape((LANES, model), f32), vmem),
+        (shape((length, model), low), vmem),
+        (shape((length, width), f32), anywhere),
+        (shape((length, width), f32), anywhere),
+        (shape((length, width), low), vmem),
+        (shape((length, width), f32), vmem),
+        (shape(waves, f32), anywhere),
+        (shape(waves, f32), anywhere),
+        (shape(waves, f32), anywhere),
+        (shape(waves, f32), anywhere),
+        (shape((own_rows, model), low), vmem),
+        (shape((own_rows, model), f32), vmem),
+        (shape((2, model), f32), vmem),
+        (shape((2, own_rows, width), low), vmem),
+        (shape(owners + (hidden,), low), anywhere),
+        (shape(owners + (hidden,), low), anywhere),
+        (shape(owners + (model,), low), vmem),
+    )
     return pl.pallas_call(
         forward_body,
-        out_shape=(
-            shape(owners + (3 * width,), low),
-            shape(owners + (model,), low),
-            shape(owners + (hidden,), low),
-            shape(owners + (hidden,), low),
-            shape((LANES, model), f32),
-            shape((length, model), low),
-            shape((length, 3 * width), f32),
-            shape((2, own_rows, width), low),
-            shape((length, width), low),
-            shape((length, width), f32),
-        )
-        + (shape(waves, f32),) * 4,
-        in_specs=[vmem, vmem, anywhere, anywhere, vmem, vmem, vmem, vmem],
-        out_specs=(vmem, anywhere, anywhere, anywhere) + (vmem,) * 10,
+        out_shape=tuple(out for out, _ in outs),
+        in_specs=[vmem, vmem, vmem, anywhere, vmem, vmem, vmem, vmem],
+        out_specs=tuple(spec for _, spec in outs),
         scratch_shapes=[
+            pltpu.VMEM((owned, 3 * width), low),
             pltpu.VMEM((2, own_rows, model), low),
             pltpu.VMEM((16,) + small.shape, low),
             pltpu.VMEM((2, own_rows, width), low),
-            pltpu.VMEM((length, width), f32),
-            pltpu.VMEM(waves, low),
-            pltpu.VMEM(waves, low),
-            pltpu.VMEM(waves, f32),
+            pltpu.VMEM((2, own_rows, width), low),
+            pltpu.VMEM(owners + (model,), low),
+            pltpu.VMEM((own_rows, width), low),
             dma((count,)),
-            dma((count + 1, 3)),
-            dma((count + 1, 3)),
-            dma((count + 1,)),
-            dma((count + 1,)),
-            dma((count + 1,)),
-            dma((count + 1,)),
-            dma((count + 1,)),
-            dma((count + 1,)),
+            dma((count, 3)),
+            dma((count, 3)),
+            dma((count,)),
+            dma((count,)),
+            dma((count,)),
+            dma((count,)),
+            dma((count,)),
+            dma((count,)),
             dma((16,)),
             dma((16,)),
-            dma((2,)),
-            dma((2,)),
+            dma((3,)),
+            dma((3,)),
+            dma((6,)),
+            dma((2, 2)),
         ],
         compiler_params=pltpu.CompilerParams(collective_id=2, has_side_effects=True, vmem_limit_bytes=VMEM_LIMIT),
-        name="forward_mixer",
-    )(tokens, qkv_shard, out_shard, mlp_shard, small, ssm, to_table, from_table)
+        name="forward_layer",
+    )(tokens, cotangent, attn_shard, mlp_shard, small, ssm, to_table, from_table)
 
 
 PIECES = (
@@ -912,7 +1142,7 @@
     ("up", 0, 1536, "whole"),
     ("qkv", 0, 1152, "apart"),
 )
-QKV = len(PIECES) - 1
+D0, U1, D1, OUT, U0, QKV = range(len(PIECES))
 
 
 def add_blocks(put, sources, count):
@@ -933,9 +1163,9 @@
 def backward_body(*refs):
     count = len(PIECES)
     (
-        gated_grad_ref, proj_ref, conv_ref, shifted_ref, kernel_w, taps_w, keys_w, mixed_w, ssm_ref, to_ref, from_ref,
+        grad_all, query_hbm, value_hbm, conv_ref, shifted_ref, kernel_w, taps_w, keys_w, mixed_w, ssm_ref, to_ref, from_ref,
         normed_ref, qkv_ref, token_ref, residual_ref, small_t, norm_two_ref, down_ref, up_ref, out_ref,
-    ), refs = refs[:20], refs[20:]
+    ), refs = refs[:21], refs[21:]
     outs, refs = refs[:count], refs[count:]
     (small_out, ssm_out, input_out), refs = refs[:3], refs[3:]
     near, refs = refs[:count], refs[count:]
@@ -944,10 +1174,10 @@
     from_y, from_z, final, last = (refs[i * count : (i + 1) * count] for i in range(4))
     refs = refs[4 * count :]
     (
-        own_ref, grad_all, query_ref, value_ref, spectrum, line_ref, decay_ref, wave_ref, high_ref, back_ref,
+        own_ref, query_ref, value_ref, spectrum, line_ref, decay_ref, wave_ref, high_ref, back_ref,
         grad_proj, qkv_grad, gn_send, gn_own, gn_last, small_rows, small_ref, small_all, small_sum, small_last,
         ssm_ref_all, ssm_all, ssm_sum,
-    ), refs = refs[:23], refs[23:]
+    ), refs = refs[:22], refs[22:]
     (
         load_sem, own_sem, core_s, core_r, x_s, x_r, y_s, y_r, z_s, z_r, f_s, f_r, sm_s, sm_r, ss_s, ss_r, sg_s, sg_r,
         side_s, side_r,
@@ -1008,10 +1238,6 @@
                 near[k][h, i // 2, i % 2] = total.astype(jnp.bfloat16)
 
             add_blocks(put, [own, lambda i, h=h: near[k][h, i // 2, i % 2]], 8)
-        if piece_halves(k) == TWO:
-            x_copy(k).start()
-        else:
-            y_copy(k).start()
 
     def add_x(k):
         x_copy(k).wait_recv()
@@ -1020,7 +1246,6 @@
             kept(k)[i // 2, i % 2] = total.astype(jnp.bfloat16)
 
         add_blocks(put, [lambda i: kept(k)[i // 2, i % 2], lambda i: from_x[k][i // 2, i % 2]], 8)
-        y_copy(k).start()
 
     def add_y(k):
         y_copy(k).wait_recv()
@@ -1029,6 +1254,8 @@
             kept(k)[i, place.y] = total.astype(jnp.bfloat16)
 
         add_blocks(put, [lambda i: kept(k)[i, place.y], lambda i: from_y[k][i]], 4)
+
+    def start_z(k):
         for step in range(1, 4):
             z_copy(k, step).start()
 
@@ -1039,7 +1266,6 @@
         for step in range(3):
             total = total + from_z[k][step].astype(jnp.float32)
         final[k][...] = total.astype(jnp.bfloat16)
-        last_copy(k).start()
 
     def finish(k):
         last_copy(k).wait_recv()
@@ -1068,10 +1294,6 @@
         other = (place.d + step) % 16
         return send(ssm_sum.at[place.d], ssm_sum.at[place.d], sg_s.at[other], sg_r.at[place.d], place.owner(other))
 
-    grad_copy = send(
-        gated_grad_ref.at[:, pl.ds(pl.multiple_of((1 - place.s) * width, LANES), width)], grad_all.at[place.s],
-        side_s.at[0], side_r.at[0], place.over_x(),
-    )
     gn_copy = send(gn_send, gn_last, side_s.at[1], side_r.at[1], place.over_x())
     small_copy = send(small_sum, small_last, side_s.at[2], side_r.at[2], place.over_x())
     spectra = (kernel_w, mixed_w, taps_w, keys_w)
@@ -1079,25 +1301,31 @@
     def load_spectrum(i):
         return pltpu.make_async_copy(spectra[i], spectrum.at[i % 2], load_sem.at[i % 2])
 
-    query_copy = pltpu.make_async_copy(proj_ref.at[:, pl.ds(0, width)], query_ref, load_sem.at[2])
-    value_copy = pltpu.make_async_copy(proj_ref.at[:, pl.ds(2 * width, width)], value_ref, load_sem.at[3])
+    query_copy = pltpu.make_async_copy(query_hbm, query_ref, load_sem.at[2])
+    value_copy = pltpu.make_async_copy(value_hbm, value_ref, load_sem.at[3])
 
     greet_all(place)
-    grad_copy.start()
-    for k in range(QKV):
+    for k in (0, 1):
         for h in range(piece_halves(k)):
             core_copy(k, h).start()
-    load_own(0)
-    load_own(1)
+        load_own(k)
     query_copy.start()
     value_copy.start()
     load_spectrum(0).start()
     load_spectrum(1).start()
-    grad_all[place.s] = gated_grad_ref[:, pl.ds(pl.multiple_of(place.s * width, LANES), width)]
-    for k in range(QKV):
-        add_core(k)
-        if k + 2 < QKV:
-            load_own(k + 2)
+    add_core(D0)
+    y_copy(D0).start()
+    for k in range(2, QKV):
+        for h in range(piece_halves(k)):
+            core_copy(k, h).start()
+    load_own(2)
+    add_core(U1)
+    x_copy(U1).start()
+    load_own(3)
+    add_core(D1)
+    load_own(4)
+    add_core(OUT)
+    add_core(U0)
 
     def keep(wave, value):
         wave_ref[wave] = value
@@ -1116,9 +1344,10 @@
 
     query_copy.wait()
     value_copy.wait()
-    grad_copy.wait_recv()
     to_waves(width, read_conv_grad, RADIX, to_ref, high_ref, None, keep)
-    add_y(0)
+    add_y(D0)
+    start_z(D0)
+    y_copy(D1).start()
     load_spectrum(0).wait()
     product(width, spectrum.at[0], wave_ref, True, high_ref, None)
     load_spectrum(2).start()
@@ -1130,7 +1359,6 @@
         line_ref[rows, cols] = gradient * value_ref[rows, cols]
 
     from_waves(width, from_ref, high_ref, None, back_ref, put_mixed)
-    add_x(1)
     load_spectrum(1).wait()
     product(width, spectrum.at[1], wave_ref, True, high_ref, None)
     load_spectrum(3).start()
@@ -1139,9 +1367,13 @@
         decay_ref[pl.ds(base + row, 16), cols] = value
 
     from_waves(width, from_ref, high_ref, None, back_ref, put_kernel)
-    add_y(2)
+    add_x(U1)
+    x_copy(OUT).start()
     to_waves(width, lines, RADIX, to_ref, high_ref, None, keep)
-    add_z(0)
+    add_y(D1)
+    y_copy(U0).start()
+    add_z(D0)
+    start_z(D1)
     load_spectrum(2).wait()
     product(width, spectrum.at[0], wave_ref, True, high_ref, None)
 
@@ -1149,7 +1381,7 @@
         grad_proj[pl.ds(base + row, 16), column(1, cols)] = value.astype(jnp.bfloat16)
 
     from_waves(width, from_ref, high_ref, None, back_ref, put_keys)
-    add_x(3)
+    add_x(OUT)
 
     def project_back(begin, put):
         def one(index, carry):
@@ -1179,27 +1411,33 @@
         )
         qkv_grad[2 * pair : 2 * pair + 2] = value.astype(jnp.bfloat16).reshape((2,) + qkv_grad.shape[1:])
     core_copy(QKV, 0).start()
-    add_y(4)
     project_back(place.s * own_rows, put_own)
+    add_y(U0)
+    y_copy(U1).start()
     add_core(QKV)
-    add_y(1)
+    add_z(D1)
+    start_z(U0)
     load_spectrum(3).wait()
     product(width, spectrum.at[1], wave_ref, True, high_ref, None)
     small_rows[...] = jnp.zeros(small_rows.shape, jnp.float32)
     small_rows[:TAP_ROWS, pl.ds(pl.multiple_of(place.s * width, LANES), width)] = first_positions(
         width, TAP_ROWS, from_ref, high_ref, None
     )
-    add_z(2)
-    add_y(3)
     decay_gradients(0, length, ssm_ref, decay_ref, ssm_ref_all)
+    add_y(U1)
+    y_copy(QKV).start()
+    add_z(U0)
+    start_z(U1)
+    decay_gradients(1, length, ssm_ref, decay_ref, ssm_ref_all)
     add_y(QKV)
-    add_z(4)
-    decay_gradients(1, length, ssm_ref, decay_ref, ssm_ref_all)
-    add_z(1)
-    add_z(3)
+    start_z(QKV)
+    y_copy(OUT).start()
+    add_z(U1)
     decay_gradients(2, length, ssm_ref, decay_ref, ssm_ref_all)
     over_peers(lambda step: to_peer(ssm_ref_all, ssm_all, ss_s, ss_r, step).start())
     gn_copy.wait_recv()
+    for k in (D0, D1, U0, U1):
+        last_copy(k).start()
 
     def norm_back(index, sums):
         rows = pl.ds(pl.multiple_of(index * 32, 32), 32)
@@ -1216,7 +1454,10 @@
     small_rows[TAP_ROWS + 2 : TAP_ROWS + 4, :] = norm_two_ref[...]
     small_ref[...] = small_rows[...].T.astype(jnp.bfloat16).reshape(small_ref.shape)
     over_peers(lambda step: to_peer(small_ref, small_all, sm_s, sm_r, step).start())
+    add_y(OUT)
+    start_z(OUT)
     add_z(QKV)
+    last_copy(QKV).start()
 
     over_peers(lambda step: from_peer(ssm_all, ss_s, ss_r, step).wait_recv())
     ssm_all[place.d] = ssm_ref_all[place.d]
@@ -1232,6 +1473,8 @@
 
     small_sum[...] = lax.fori_loop(1, 16, add_small, small_ref[place.d].astype(jnp.float32)).astype(jnp.bfloat16)
     small_copy.start()
+    add_z(OUT)
+    last_copy(OUT).start()
     for k in range(count):
         finish(k)
     over_peers(lambda step: from_peer(ssm_sum, sg_s, sg_r, step).wait_recv())
@@ -1248,7 +1491,7 @@
         for step in range(1, 4):
             z_copy(k, step).wait_send()
         last_copy(k).wait_send()
-    for copy in (grad_copy, gn_copy, small_copy):
+    for copy in (gn_copy, small_copy):
         copy.wait_send()
     over_peers(lambda step: to_peer(small_ref, small_all, sm_s, sm_r, step).wait_send())
     over_peers(lambda step: to_peer(ssm_ref_all, ssm_all, ss_s, ss_r, step).wait_send())
@@ -1256,7 +1499,7 @@
 
 
 def backward_mixer(
-    gated_grad, proj, conv, shifted, kernel_w, taps_w, keys_w, mixed_w, ssm, to_table, from_table, normed, qkv, tokens,
+    gated_grad, query, value, conv, shifted, kernel_w, taps_w, keys_w, mixed_w, ssm, to_table, from_table, normed, qkv, tokens,
     residual, small, norm_two, down, up, out,
 ):
     f32, low = jnp.float32, jnp.bfloat16
@@ -1290,7 +1533,7 @@
     return pl.pallas_call(
         backward_body,
         out_shape=tuple(results),
-        in_specs=[vmem, anywhere, vmem, vmem] + [anywhere] * 4 + [vmem] * 9 + [anywhere] * 3,
+        in_specs=[vmem, anywhere, anywhere, vmem, vmem] + [anywhere] * 4 + [vmem] * 9 + [anywhere] * 3,
         out_specs=(vmem,) * len(results),
         scratch_shapes=near
         + from_x
@@ -1300,7 +1543,6 @@
         + last
         + [
             pltpu.VMEM((2, FOUR, TWO, owned, 1536), low),
-            pltpu.VMEM((2, own_rows, width), low),
             pltpu.VMEM((length, width), f32),
             pltpu.VMEM((length, width), f32),
             pltpu.VMEM((2,) + waves, f32),
@@ -1335,9 +1577,85 @@
         compiler_params=pltpu.CompilerParams(collective_id=1, has_side_effects=True, vmem_limit_bytes=VMEM_LIMIT),
         name="backward_mixer",
     )(
-        gated_grad, proj, conv, shifted, kernel_w, taps_w, keys_w, mixed_w, ssm, to_table, from_table, normed, qkv, tokens,
+        gated_grad, query, value, conv, shifted, kernel_w, taps_w, keys_w, mixed_w, ssm, to_table, from_table, normed, qkv, tokens,
         residual, small, norm_two, down, up, out,
     )
+
+
+def adam_parts(param, first, second, gradient, learn_rate, decay_weight):
+    first_new = BETA_ONE * first + (1.0 - BETA_ONE) * gradient
+    second_new = BETA_TWO * second + (1.0 - BETA_TWO) * gradient * gradient
+    first_hat = first_new / (1.0 - BETA_ONE**STEP_COUNT)
+    second_hat = second_new / (1.0 - BETA_TWO**STEP_COUNT)
+    step = learn_rate * (first_hat / (jnp.sqrt(second_hat) + ADAM_EPS) + decay_weight * param)
+    return step, first_new, second_new
+
+
+def adam_body(
+    down_first, up_last, down_last, out_sum, up_first, qkv_sum, small_sum, ssm_sum,
+    attn_p, mlp_p, norm_p, tap_p, ssm_p, attn_m, mlp_m, norm_m, tap_m, ssm_m,
+    attn_step, attn_new, mlp_step, mlp_new, norm_step, norm_new, tap_step, tap_new, ssm_step, ssm_new,
+    *, scale,
+):
+    f32 = jnp.float32
+    width = out_sum.shape[2]
+
+    def attn(start, gradient):
+        cols = slice(start, start + width)
+        attn_step[:, cols], attn_new[0, :, cols], attn_new[1, :, cols] = adam_parts(
+            attn_p[:, cols].astype(f32), attn_m[0, :, cols], attn_m[1, :, cols], gradient.astype(f32) * scale,
+            LEARN_RATE, DECAY_RATE,
+        )
+
+    def mlp(plane, start, source, slot):
+        count = source.shape[-1]
+        for begin in range(0, count, width):
+            gradient = source[:, begin : begin + width] if slot is None else source[slot, :, begin : begin + width]
+            cols = slice(start + begin, start + begin + width)
+            mlp_step[plane, :, cols], mlp_new[0, plane, :, cols], mlp_new[1, plane, :, cols] = adam_parts(
+                mlp_p[plane, :, cols].astype(f32), mlp_m[0, plane, :, cols], mlp_m[1, plane, :, cols],
+                gradient.astype(f32) * scale, LEARN_RATE, DECAY_RATE,
+            )
+
+    for half in range(2):
+        for place in range(3):
+            attn((2 * place + half) * width, qkv_sum[half, :, place * width : (place + 1) * width])
+        attn((6 + half) * width, out_sum[half])
+        mlp(0, up_first.shape[1] + half * up_last.shape[2], up_last, half)
+    mlp(0, 0, up_first, None)
+    mlp(1, 0, down_first, None)
+    mlp(1, down_first.shape[1], down_last, None)
+    tap_step[...], tap_new[0], tap_new[1] = adam_parts(
+        tap_p[...].astype(f32), tap_m[0], tap_m[1], small_sum[:, :TAP_ROWS] * scale, LEARN_RATE, DECAY_RATE
+    )
+    small = small_sum[...].T * scale
+    norm_step[...], norm_new[0], norm_new[1] = adam_parts(
+        norm_p[...].astype(f32), norm_m[0], norm_m[1], small[TAP_ROWS : TAP_ROWS + 4], LEARN_RATE, 0.0
+    )
+    for plane in range(2):
+        gradient = ssm_sum[plane * 8 : plane * 8 + 8].reshape(ssm_p.shape[1:]) * scale
+        ssm_step[plane], ssm_new[0, plane], ssm_new[1, plane] = adam_parts(
+            ssm_p[plane], ssm_m[0, plane], ssm_m[1, plane], gradient, SSM_LEARN_RATE, 0.0
+        )
+
+
+def adam_all(sums, params, moments, scale):
+    vmem = pl.BlockSpec(memory_space=pltpu.VMEM)
+    outs = []
+    for param, moment in zip(params, moments):
+        outs += [jax.ShapeDtypeStruct(param.shape, jnp.float32), jax.ShapeDtypeStruct(moment.shape, jnp.float32)]
+    return pl.pallas_call(
+        partial(adam_body, scale=scale),
+        out_shape=tuple(outs),
+        in_specs=[vmem] * (len(sums) + 2 * len(params)),
+        out_specs=(vmem,) * len(outs),
+        compiler_params=pltpu.CompilerParams(vmem_limit_bytes=VMEM_LIMIT),
+        name="adam",
+    )(*sums, *params, *moments)
+
+
+def turned_last(value):
+    return jnp.swapaxes(value, -1, -2)
 
 
 def per_device_split(
@@ -1360,76 +1678,35 @@
     owners = lax.axis_size("dp")
     length = rows * shares
     part = width // shares
-    half = lax.axis_index("seq")
     tap_count = taps.shape[0]
     to_table, from_table = map(jnp.asarray, transform_tables())
 
     owned = attn_weight.shape[0]
-    columns = lax.dynamic_index_in_dim(attn_weight.reshape(owned, 4, shares, part), half, 2, False)
-    qkv_shard = columns[:, :3].reshape(owned, 3 * part)
     small = jnp.concatenate([taps, norms, jnp.zeros((LANES - 4 - tap_count, owned), low)]).T
     ssm_turned = jnp.swapaxes(ssm_params, 1, 2)
     (
-        qkv_full, out_full, up_full, down_full, small_full, normed_low, proj, gated_parts,
-        conv, shifted, kernel_w, taps_w, keys_w, mixed_w,
-    ) = forward_mixer(
-        tokens[0], qkv_shard, attn_weight[:, 3 * width :], mlp_weight, small, ssm_turned, to_table, from_table
-    )
-    qkv_full = qkv_full.reshape(width, 3 * part)
-    out_full = out_full.reshape(width, width)
-    mlp_full = (up_full.reshape(width, -1), down_full.reshape(width, -1))
-    norm_rows = small_full[tap_count : tap_count + 4]
-    gated_rows = jnp.concatenate([gated_parts[0], gated_parts[1]], axis=1)
-    inputs = tokens[0].astype(f32)
-    residual = inputs + dot(gated_rows, out_full)
-    normal_two, inverse_two = layer_norm_parts(residual)
-    normed_two = (normal_two * norm_rows[2] + norm_rows[3]).astype(low)
-    before = dot(normed_two, mlp_full[0])
-    active, gelu_pull = jax.vjp(jax.nn.gelu, before)
-    active_low = active.astype(low)
-    grad_after = cotangent[0]
-    layer_out = (
-        residual + jnp.einsum("tf,df->td", active_low, mlp_full[1], preferred_element_type=f32)
-    ).astype(low)
-    grad_active = dot(grad_after, mlp_full[1])
-    grad_down = jnp.einsum("td,tf->df", grad_after, active_low, preferred_element_type=f32)
-    grad_before = gelu_pull(grad_active)[0].astype(low)
-    grad_up = jnp.einsum("td,tf->df", normed_two, grad_before, preferred_element_type=f32)
-    grad_normed_two = jnp.einsum("tf,df->td", grad_before, mlp_full[0], preferred_element_type=f32)
-    into_two, gain_two, bias_two = layer_norm_back(grad_normed_two, normal_two, inverse_two, norm_rows[2])
-    grad_residual = grad_after.astype(f32) + into_two
-    grad_branch = grad_residual.astype(low)
-    grad_out = jnp.einsum("td,te->de", gated_rows, grad_branch, preferred_element_type=f32)
-    grad_gated = jnp.einsum("te,de->td", grad_branch, out_full, preferred_element_type=f32).astype(low)
-
-    def by_owner(gradient):
-        return gradient.astype(low).reshape(FOUR, TWO, TWO, owned, gradient.shape[1])
-
+        qkv_full, _, _, small_full, normed_low, query, value, conv, shifted, kernel_w, taps_w, keys_w, mixed_w,
+        layer_out, grad_residual, grad_norm_two, grad_gated, grad_up, grad_down, grad_out,
+    ) = forward_layer(
+        tokens[0], cotangent[0], attn_weight, mlp_weight, small, ssm_turned,
+        to_table, from_table,
+    )
     scale = 1.0 / math.sqrt(owners * length)
     sums = backward_mixer(
-        grad_gated, proj, conv, shifted, kernel_w, taps_w, keys_w, mixed_w, ssm_turned, to_table, from_table,
-        normed_low, qkv_full, tokens[0], grad_residual, small_full, jnp.concatenate([gain_two, bias_two]),
-        by_owner(grad_down), by_owner(grad_up), by_owner(grad_out),
-    )
-    down_sum = jnp.concatenate([sums[0], sums[2]], axis=1)
-    up_sum = jnp.concatenate([sums[4], sums[1][0].astype(f32), sums[1][1].astype(f32)], axis=1)
-    qkv_sum = jnp.swapaxes(sums[5].reshape(shares, owned, 3, part), 0, 1).swapaxes(1, 2)
-    attn_sum = jnp.concatenate([qkv_sum.reshape(owned, 3 * width), sums[3][0], sums[3][1]], axis=1)
-    mlp_sum = jnp.stack([up_sum, down_sum])
-    small_sum = sums[6].T
-    small_sum = jnp.concatenate([small_sum[tap_count : tap_count + 4], small_sum[:tap_count]])
-    ssm_sum = jnp.swapaxes(sums[7].reshape(ssm_turned.shape), 1, 2)
+        grad_gated, query, value, conv, shifted, kernel_w, taps_w, keys_w, mixed_w, ssm_turned, to_table, from_table,
+        normed_low, qkv_full.reshape(width, 3 * part), tokens[0], grad_residual, small_full, grad_norm_two,
+        grad_down, grad_up, grad_out,
+    )
+    (
+        attn_step, attn_new, mlp_step, mlp_new, norms_step, norm_new, taps_step, tap_new, ssm_step, ssm_new
+    ) = adam_all(
+        sums[:8],
+        (attn_weight, mlp_weight, norms, taps.T, ssm_turned),
+        (attn_moments, mlp_moments, norm_moments, turned_last(tap_moments), turned_last(ssm_moments)),
+        scale,
+    )
+    taps_step, tap_new, ssm_step, ssm_new = map(turned_last, (taps_step, tap_new, ssm_step, ssm_new))
     input_grad = sums[8]
-
-    attn_step, attn_new = adam_update(
-        attn_weight.astype(f32), attn_moments, attn_sum.astype(f32) * scale, LEARN_RATE, DECAY_RATE
-    )
-    mlp_step, mlp_new = adam_update(
-        mlp_weight.astype(f32), mlp_moments, mlp_sum.astype(f32) * scale, LEARN_RATE, DECAY_RATE
-    )
-    norms_step, norm_new = adam_update(norms.astype(f32), norm_moments, small_sum[:4] * scale, LEARN_RATE, 0.0)
-    taps_step, tap_new = adam_update(taps.astype(f32), tap_moments, small_sum[4:] * scale, LEARN_RATE, DECAY_RATE)
-    ssm_step, ssm_new = adam_update(ssm_params, ssm_moments, ssm_sum * scale, SSM_LEARN_RATE, 0.0)
     return (
         layer_out[None],
         input_grad[None],

time: 271 us -> 245 us (0.904)
  matrix products: 32.3 us -> 0 us
  Pallas kernels: 212 us -> 239 us
  other arithmetic: 12.6 us -> 1.39 us
  local copies, waits for them, and re-layouts: 12.5 us -> 3.68 us
    dot_general x9 -> x0, matrix products: 32.3 us -> none  [the longest x3 11.3 us: dot(): return jnp.dot(left, right, preferred_element_type=jnp.float32)]
    pallas_call x1 -> x2, Pallas kernels: 104 us -> 130 us  [the longest x1 124 us: forward_layer(): pl.pallas_call(forward_body, out_shape=tuple((out for out, _ in outs)), i...]
    another operation x9 -> x0, other arithmetic: 6.32 us -> none  [the longest x8 6.23 us: adam_update(): return (step_size, jnp.stack([first_new, second_new]))]
    mul x4 -> x0, other arithmetic: 3.29 us -> none  [the longest x3 3.25 us: adam_update(): learn_rate * (first_hat / (jnp.sqrt(second_hat) + ADAM_EPS) + decay_weigh...]
    reshape x4 -> x0, local copies, waits for them, and re-layouts: 3.01 us -> none  [the longest x1 1.21 us: per_device_split(): attn_weight.reshape(owned, 4, shares, part)]
where the time goes in v1:
time: 245 us
  Pallas kernels  239 us (98%)
  local copies, waits for them, and re-layouts  3.68 us (2%)
    pallas_call x1, Pallas kernels, forward_layer(): pl.pallas_call(forward_body, out_shape=tuple((out for out, _ in outs)), i...  124 us
    pallas_call x1, Pallas kernels, backward_mixer(): pl.pallas_call(backward_body, out_shape=tuple(results), in_specs=[vmem, a...  109 us
    pallas_call x1, Pallas kernels, adam_all(): pl.pallas_call(partial(adam_body, scale=scale), out_shape=tuple(outs), in...  6.22 us

profile of v1, /device:TPU:0, one launch (start us, length us, event | category | flops | bytes accessed | tf_op | source)
XLA Modules:
  0.0 245.1 jit_solution(1926871299436338113)
XLA Ops:
  0.7 0.1 pad.2.clone
  0.7 0.8 copy.26
  1.5 1.4 maximum_bitcast_fusion.small_ref
  2.9 124.3 %forward_layer.1 = (bf16[4,2,2,48,1152]{4,3,2,1,0:T(8,128)(2,1)}, bf16[4,2,2,48,3072]{4,3,2,1,0:T(8,128)(2,1)}, bf16[4,2,2,48,3072]{4,3,2,1,0:T(8,128)(2,1)}, f3...) custom-call(bf16[512,768]{1,0:T(8,128)(2,1)} %bitcast.15, ...), custom_call_target="tpu_custom_call" | custom-call | tf_op jit(solution)/shard_map/forward_layer/pallas_call | solution.py:1103
  127.2 108.9 %backward_mixer.1 = (f32[48,1536]{1,0:T(8,128)}, bf16[2,48,768]{2,1,0:T(8,128)(2,1)}, f32[48,1536]{1,0:T(8,128)}, bf16[2,48,384]{2,1,0:T(8,128)(2,1)}, f32[48,15...) custom-call(bf16[2,512,384]{2,1,0:T(8,128)(2,1)} %get-tuple-element., ...), custom_call_target="tpu_custom_call" | custom-call | tf_op jit(solution)/shard_map/backward_mixer/pallas_call | solution.py:1533
  236.1 0.0 copy-start.1
  236.1 6.2 %adam.1 = (f32[48,3072]{1,0:T(8,128)}, f32[2,48,3072]{2,1,0:T(8,128)}, f32[2,48,3072]{2,1,0:T(8,128)}, f32[2,2,48,3072]{3,2,1,0:T(8,128)}, f32[4,48]{1,0:T(4,128...) custom-call(f32[48,1536]{1,0:T(8,128)} %get-tuple-element.68.down_fi, ...), custom_call_target="tpu_custom_call" | custom-call | tf_op jit(solution)/shard_map/adam/pallas_call | solution.py:1647
  242.3 0.0 copy-start
  242.3 0.0 copy-done.1
  242.3 0.9 copy.29
  243.2 0.8 copy-done
  244.0 1.1 copy.30
  (1 shorter events, 0.0 us)
Async XLA Ops:
  236.1 6.2 %copy-start.1 = (bf16[512,768]{1,0:T(8,128)(2,1)S(1)}, bf16[512,768]{1,0:T(8,128)(2,1)}, u32[]{:S(2)}) copy-start(bf16[512,768]{1,0:T(8,128)(2,1)} %get-tuple-element.49) | copy-start | bytes 2359300
  242.3 1.7 copy-start

commit v2 on v1

--- a/solution.py
+++ b/solution.py
@@ -488,34 +488,33 @@
 FINE = 32
 
 
-def decay_sums(width, length, ssm_ref, out_ref):
+def decay_sums(block, length, ssm_ref, out_ref):
     modes = ssm_ref.shape[1]
     steps = length // FINE
-    out_ref[...] = jnp.zeros(out_ref.shape, jnp.float32)
-    for block in range(width // LANES):
-        cols = pl.ds(block * LANES, LANES)
-        offsets = lax.broadcasted_iota(jnp.int32, (FINE, LANES), 0).astype(jnp.float32)
-
-        def group(index, carry, cols=cols, offsets=offsets):
-            base = pl.multiple_of(index * 8, 8)
-            rates = jnp.exp(ssm_ref[0, pl.ds(base, 8), cols])
-            leaps = jnp.exp(-rates * FINE)
-            weights = ssm_ref[1, pl.ds(base, 8), cols]
-            terms = tuple(weights[i : i + 1] * jnp.exp(-rates[i : i + 1] * offsets) for i in range(8))
-            leap_rows = [jnp.broadcast_to(leaps[i : i + 1], (FINE, LANES)) for i in range(8)]
-
-            def step(number, terms, leap_rows=leap_rows):
-                rows = pl.ds(pl.multiple_of(number * FINE, FINE), FINE)
-                total = out_ref[rows, cols]
-                for term in terms:
-                    total = total + term
-                out_ref[rows, cols] = total
-                return tuple(term * leap for term, leap in zip(terms, leap_rows))
-
-            lax.fori_loop(0, steps, step, terms, unroll=4)
-            return carry
-
-        lax.fori_loop(0, modes // 8, group, 0)
+    cols = pl.ds(block * LANES, LANES)
+    out_ref[:, cols] = jnp.zeros((length, LANES), jnp.float32)
+    offsets = lax.broadcasted_iota(jnp.int32, (FINE, LANES), 0).astype(jnp.float32)
+
+    def group(index, carry):
+        base = pl.multiple_of(index * 8, 8)
+        rates = jnp.exp(ssm_ref[0, pl.ds(base, 8), cols])
+        leaps = jnp.exp(-rates * FINE)
+        weights = ssm_ref[1, pl.ds(base, 8), cols]
+        terms = tuple(weights[i : i + 1] * jnp.exp(-rates[i : i + 1] * offsets) for i in range(8))
+        leap_rows = [jnp.broadcast_to(leaps[i : i + 1], (FINE, LANES)) for i in range(8)]
+
+        def step(number, terms):
+            rows = pl.ds(pl.multiple_of(number * FINE, FINE), FINE)
+            total = out_ref[rows, cols]
+            for term in terms:
+                total = total + term
+            out_ref[rows, cols] = total
+            return tuple(term * leap for term, leap in zip(terms, leap_rows))
+
+        lax.fori_loop(0, steps, step, terms, unroll=4)
+        return carry
+
+    lax.fori_loop(0, modes // 8, group, 0)
 
 
 def decay_gradients(block, length, ssm_ref, grad_ref, out_ref):
@@ -616,15 +615,28 @@
     pl.semaphore_wait(barrier, 16)
 
 
+def add_blocks(put, sources, count):
+    def one(index, carry):
+        total = sources[0](index).astype(jnp.float32)
+        for source in sources[1:]:
+            total = total + source(index).astype(jnp.float32)
+        put(index, total)
+        return carry
+
+    lax.fori_loop(0, count, one, 0)
+
+
 WEIGHTS = (
     ("out", 0, 768, "whole"),
     ("up", 0, 1536, "halved"),
     ("down", 0, 1536, "whole"),
     ("up", 1536, 1536, "halved"),
-    ("down", 1536, 1536, "whole"),
+    ("down", 1536, 768, "whole"),
+    ("down", 2304, 768, "whole"),
 )
-OUT_W, UP_FIRST, DOWN_FIRST, UP_LAST, DOWN_LAST, QKV_W = range(len(WEIGHTS) + 1)
+OUT_W, UP_FIRST, DOWN_FIRST, UP_LAST, DOWN_THIRD, DOWN_LAST, QKV_W = range(len(WEIGHTS) + 1)
 HIDDEN_BLOCK = 768
+EARLY = 1
 
 
 def dot_right(left, right):
@@ -646,9 +658,9 @@
 def forward_body(
     token_ref, cotangent_ref, attn_shard, mlp_shard, small_ref, ssm_ref, to_ref, from_ref,
     qkv_full, up_full, down_full, small_t, normed_ref, query_out, value_out, conv_ref, shifted_ref,
-    kernel_out, taps_out, keys_out, mixed_out, layer_out, residual_grad, norm_two_out, gated_grad, up_grad, down_grad, out_grad,
-    qkv_ref, token_all, small_all, gated_ref, rows_ref, out_full, grad_send,
-    own_sem, z_s, z_r, y_s, y_r, x_s, x_r, core_s, core_r, small_s, small_r, side_s, side_r, store_sem, load_sem,
+    kernel_out, taps_out, keys_out, mixed_out, layer_out, residual_grad, norm_two_out, gated_grad, up_grad, down_grad, out_grad, early_out,
+    qkv_ref, token_all, small_all, gated_ref, rows_ref, out_full, grad_send, near, from_y, from_z, final, last,
+    own_sem, z_s, z_r, y_s, y_r, x_s, x_r, core_s, core_r, small_s, small_r, side_s, side_r, store_sem, load_sem, nc_s, nc_r, ny_s, ny_r, nz_s, nz_r, nf_s, nf_r,
 ):
     length, width = conv_ref.shape
     own_rows, model = token_ref.shape
@@ -727,30 +739,62 @@
     gated_copy = send(gated_ref.at[1 - place.s], rows_ref.at[place.s], side_s.at[1], side_r.at[1], place.over_x())
     grad_copy = send(grad_send, gated_grad.at[place.s], side_s.at[2], side_r.at[2], place.over_x())
 
+    def early_y(e):
+        return send(near.at[e, :, 1 - place.y], from_y.at[e], ny_s.at[e], ny_r.at[e], place.over_y())
+
+    def early_z(e, step):
+        other = (place.z + step) % 4
+        return send(
+            near.at[e, other, place.y], from_z.at[e, step - 1], nz_s.at[e, step - 1], nz_r.at[e, step - 1],
+            place.along_z(step),
+        )
+
+    def early_last(e):
+        return send(final.at[e], last.at[e], nf_s.at[e], nf_r.at[e], place.over_x())
+
+    def early_add_y(e):
+        early_y(e).wait_recv()
+
+        def put(i, total):
+            near[e, i, place.y] = total.astype(low)
+
+        add_blocks(put, [lambda i: near[e, i, place.y], lambda i: from_y[e, i]], 4)
+        for step in range(1, 4):
+            early_z(e, step).start()
+
+    def early_add_z(e):
+        for step in range(1, 4):
+            early_z(e, step).wait_recv()
+        total = near[e, place.z, place.y].astype(f32)
+        for step in range(3):
+            total = total + from_z[e, step].astype(f32)
+        final[e] = total.astype(low)
+        early_last(e).start()
+
     def step_one():
         wait_z(QKV_W)
         y_copy(QKV_W).start()
-        start_z(OUT_W)
+        start_z(UP_FIRST)
+
+    def step_two():
         for copy in own_copies():
             copy.wait()
-
-    def step_two():
         wait_z(OUT_W)
-        start_z(UP_FIRST)
+        y_copy(OUT_W).start()
+        start_z(DOWN_FIRST)
 
     def step_three():
         y_copy(QKV_W).wait_recv()
         core_copy(QKV_W).start()
-        y_copy(OUT_W).start()
 
     def step_four():
         wait_z(UP_FIRST)
-        start_z(DOWN_FIRST)
+        y_copy(UP_FIRST).start()
+        start_z(UP_LAST)
 
     def step_five():
         y_copy(OUT_W).wait_recv()
         core_copy(OUT_W).start()
-        y_copy(UP_FIRST).start()
 
     def step_six():
         y_copy(UP_FIRST).wait_recv()
@@ -759,10 +803,11 @@
     def step_seven():
         wait_z(DOWN_FIRST)
         y_copy(DOWN_FIRST).start()
-        start_z(UP_LAST)
+        start_z(DOWN_THIRD)
 
     def step_eight():
         wait_z(UP_LAST)
+        y_copy(UP_LAST).start()
         start_z(DOWN_LAST)
 
     def step_nine():
@@ -772,15 +817,18 @@
     def step_ten():
         y_copy(DOWN_FIRST).wait_recv()
         core_copy(DOWN_FIRST).start()
-        y_copy(UP_LAST).start()
 
     def step_eleven():
+        wait_z(DOWN_THIRD)
+        y_copy(DOWN_THIRD).start()
         y_copy(UP_LAST).wait_recv()
         x_copy(UP_LAST).start()
 
     def step_twelve():
         wait_z(DOWN_LAST)
         y_copy(DOWN_LAST).start()
+        y_copy(DOWN_THIRD).wait_recv()
+        core_copy(DOWN_THIRD).start()
 
     def step_thirteen():
         x_copy(UP_LAST).wait_recv()
@@ -823,7 +871,10 @@
             pltpu.make_async_copy(proj_ref.at[:, pl.ds(0, width)], query_out, store_sem.at[4]),
             pltpu.make_async_copy(proj_ref.at[:, pl.ds(2 * width, width)], value_out, store_sem.at[5]),
         ]
-        decay_sums(width, length, ssm_ref, line_ref)
+        for block in range(width // LANES):
+            decay_sums(block, length, ssm_ref, line_ref)
+            if not block:
+                start_z(OUT_W)
         step_one()
         to_waves(width, lines, RADIX, to_ref, high_ref, low_ref, keep(kernel_w))
         stores[0].start()
@@ -844,7 +895,7 @@
                 normed_ref[pl.ds(pl.multiple_of(begin + row, 32), 32), :] = scaled.astype(low)
                 return carry
 
-            lax.fori_loop(0, own_rows // 32, one, 0)
+            lax.fori_loop(0, own_rows // 32, one, 0, unroll=4)
 
         def project(begin):
             weight = qkv_full[...].reshape(model, 3 * width)
@@ -864,12 +915,12 @@
         step_three()
         to_waves(width, read_taps, 1, to_ref, high_ref, low_ref, keep(other_w))
         stores[1].start()
-        step_four()
         core_copy(QKV_W).wait_recv()
         project(own_begin)
         project(other_begin)
         stores[4].start()
         stores[5].start()
+        step_four()
         step_five()
         to_waves(
             width, lambda base, row, cols: proj_ref[pl.ds(base + row, 16), column(1, cols)],
@@ -940,6 +991,20 @@
                 for i, (full, held) in enumerate(((up_grad, up_g), (down_grad, down_g)))
             ]
 
+        def early_core(e):
+            source = up_g if e % 2 else down_g
+            return send(source.at[:, :, 1 - place.c], near.at[e], nc_s.at[e], nc_r.at[e], place.over_core())
+
+        def early_add_core(e):
+            source = up_g if e % 2 else down_g
+            early_core(e).wait_recv()
+
+            def put(i, total):
+                near[e, i // 2, i % 2] = total.astype(low)
+
+            add_blocks(put, [lambda i: source[i // 2, i % 2, place.c], lambda i: near[e, i // 2, i % 2]], 8)
+            early_core(e).wait_send()
+
         step_nine()
         cot_turned[...] = cotangent_ref[...].T
         step_ten()
@@ -962,21 +1027,28 @@
             normed_two[rows, :] = scaled.astype(low)
             return carry
 
-        lax.fori_loop(0, own_rows // 32, normalize, 0)
+        lax.fori_loop(0, own_rows // 32, normalize, 0, unroll=4)
         core_copy(UP_FIRST).wait_recv()
         core_copy(DOWN_FIRST).wait_recv()
         for copy in load(0) + load(1):
             copy.start()
         normed_turned[...] = normed_two[...].T
         step_eleven()
-        step_twelve()
         for j in range(blocks):
-            if j == blocks // 2:
+            if j == 1:
+                step_twelve()
+            if j == 2:
                 step_thirteen()
+                core_copy(UP_LAST).wait_recv()
+                core_copy(DOWN_THIRD).wait_recv()
+                for copy in load(j):
+                    copy.start()
+            if j == 3:
                 step_fourteen()
-                core_copy(UP_LAST).wait_recv()
+                early_y(0).start()
+                early_y(1).start()
                 core_copy(DOWN_LAST).wait_recv()
-                for copy in load(j) + load(j + 1):
+                for copy in load(j):
                     copy.start()
             for copy in load(j):
                 copy.wait()
@@ -1000,13 +1072,20 @@
                 return carry
 
             lax.fori_loop(0, own_rows // 256, rows_of, 0)
-            if j:
+            if j == 1:
+                early_add_core(0)
+                early_add_core(1)
+            if j > EARLY:
                 for copy in store(j - 1):
                     copy.wait()
             down_g[...] = dot(cot_turned[...], active_ref[...]).astype(low).reshape(block_shape)
             up_g[...] = dot(normed_turned[...], before_ref[...]).astype(low).reshape(block_shape)
-            for copy in store(j):
-                copy.start()
+            if j < EARLY:
+                for e in (2 * j, 2 * j + 1):
+                    early_core(e).start()
+            else:
+                for copy in store(j):
+                    copy.start()
 
         def norm_back(index, sums):
             rows = pl.ds(pl.multiple_of(index * 32, 32), 32)
@@ -1021,7 +1100,7 @@
             return sums[0] + gain, sums[1] + bias
 
         zero = small_t[TAP_ROWS : TAP_ROWS + 1, :] * 0.0
-        gain, bias = lax.fori_loop(0, own_rows // 32, norm_back, (zero, zero))
+        gain, bias = lax.fori_loop(0, own_rows // 32, norm_back, (zero, zero), unroll=4)
         norm_two_out[0:1, :] = gain
         norm_two_out[1:2, :] = bias
         part_shape = (2,) + out_full.shape[1:]
@@ -1030,11 +1109,18 @@
         grad_copy.start()
         own_w = out_full[pl.ds(2 * place.s, 2)].reshape(width, model)
         gated_grad[place.s] = dot_right(active_ref[...], own_w).astype(low)
+        early_add_y(0)
+        early_add_y(1)
         for h in range(2):
             out_grad[2 * h : 2 * h + 2] = dot_left(rows_ref[h], active_ref[...]).astype(low).reshape(part_shape)
         for copy in store(blocks - 1):
             copy.wait()
+        early_add_z(0)
+        early_add_z(1)
         grad_copy.wait_recv()
+        for e in range(2 * EARLY):
+            early_last(e).wait_recv()
+            early_out[e] = final[e].astype(f32) + last[e].astype(f32)
 
     block = (FOUR, TWO, TWO, out_full.shape[3], HIDDEN_BLOCK)
     pl.run_scoped(
@@ -1053,6 +1139,11 @@
         pltpu.VMEM((own_rows, model), f32),
     )
 
+    for e in range(2 * EARLY):
+        early_y(e).wait_send()
+        for step in range(1, 4):
+            early_z(e, step).wait_send()
+        early_last(e).wait_send()
     over_peers(lambda step: small_copy(step).wait_send())
     for copy in (token_copy, gated_copy, grad_copy):
         copy.wait_send()
@@ -1099,6 +1190,7 @@
         (shape(owners + (hidden,), low), anywhere),
         (shape(owners + (hidden,), low), anywhere),
         (shape(owners + (model,), low), vmem),
+        (shape((2 * EARLY, owned, HIDDEN_BLOCK), f32), vmem),
     )
     return pl.pallas_call(
         forward_body,
@@ -1113,6 +1205,11 @@
             pltpu.VMEM((2, own_rows, width), low),
             pltpu.VMEM(owners + (model,), low),
             pltpu.VMEM((own_rows, width), low),
+            pltpu.VMEM((2 * EARLY, FOUR, TWO, owned, HIDDEN_BLOCK), low),
+            pltpu.VMEM((2 * EARLY, FOUR, owned, HIDDEN_BLOCK), low),
+            pltpu.VMEM((2 * EARLY, 3, owned, HIDDEN_BLOCK), low),
+            pltpu.VMEM((2 * EARLY, owned, HIDDEN_BLOCK), low),
+            pltpu.VMEM((2 * EARLY, owned, HIDDEN_BLOCK), low),
             dma((count,)),
             dma((count, 3)),
             dma((count, 3)),
@@ -1128,32 +1225,24 @@
             dma((3,)),
             dma((6,)),
             dma((2, 2)),
-        ],
+        ]
+        + [dma((2 * EARLY,))] * 4
+        + [dma((2 * EARLY, 3))] * 2
+        + [dma((2 * EARLY,))] * 2,
         compiler_params=pltpu.CompilerParams(collective_id=2, has_side_effects=True, vmem_limit_bytes=VMEM_LIMIT),
         name="forward_layer",
     )(tokens, cotangent, attn_shard, mlp_shard, small, ssm, to_table, from_table)
 
 
 PIECES = (
-    ("down", 0, 1536, "whole"),
+    ("down", 1536, 1536, "whole"),
     ("up", 1536, 1536, "halved"),
-    ("down", 1536, 1536, "whole"),
+    ("down", 768, 768, "whole"),
+    ("up", 768, 768, "whole"),
     ("out", 0, 768, "halved"),
-    ("up", 0, 1536, "whole"),
     ("qkv", 0, 1152, "apart"),
 )
-D0, U1, D1, OUT, U0, QKV = range(len(PIECES))
-
-
-def add_blocks(put, sources, count):
-    def one(index, carry):
-        total = sources[0](index).astype(jnp.float32)
-        for source in sources[1:]:
-            total = total + source(index).astype(jnp.float32)
-        put(index, total)
-        return carry
-
-    lax.fori_loop(0, count, one, 0)
+D1, U1, DM, UM, OUT, QKV = range(len(PIECES))
 
 
 def piece_halves(k):
@@ -1305,27 +1394,25 @@
     value_copy = pltpu.make_async_copy(value_hbm, value_ref, load_sem.at[3])
 
     greet_all(place)
-    for k in (0, 1):
+    for k in range(QKV):
         for h in range(piece_halves(k)):
             core_copy(k, h).start()
-        load_own(k)
+    load_own(D1)
+    load_own(U1)
     query_copy.start()
+    load_spectrum(0).start()
     value_copy.start()
-    load_spectrum(0).start()
     load_spectrum(1).start()
-    add_core(D0)
-    y_copy(D0).start()
-    for k in range(2, QKV):
-        for h in range(piece_halves(k)):
-            core_copy(k, h).start()
-    load_own(2)
+    add_core(D1)
+    y_copy(D1).start()
+    load_own(DM)
     add_core(U1)
     x_copy(U1).start()
-    load_own(3)
-    add_core(D1)
-    load_own(4)
+    load_own(UM)
+    add_core(DM)
+    load_own(OUT)
+    add_core(UM)
     add_core(OUT)
-    add_core(U0)
 
     def keep(wave, value):
         wave_ref[wave] = value
@@ -1345,9 +1432,6 @@
     query_copy.wait()
     value_copy.wait()
     to_waves(width, read_conv_grad, RADIX, to_ref, high_ref, None, keep)
-    add_y(D0)
-    start_z(D0)
-    y_copy(D1).start()
     load_spectrum(0).wait()
     product(width, spectrum.at[0], wave_ref, True, high_ref, None)
     load_spectrum(2).start()
@@ -1359,6 +1443,9 @@
         line_ref[rows, cols] = gradient * value_ref[rows, cols]
 
     from_waves(width, from_ref, high_ref, None, back_ref, put_mixed)
+    add_y(D1)
+    start_z(D1)
+    y_copy(DM).start()
     load_spectrum(1).wait()
     product(width, spectrum.at[1], wave_ref, True, high_ref, None)
     load_spectrum(3).start()
@@ -1370,10 +1457,10 @@
     add_x(U1)
     x_copy(OUT).start()
     to_waves(width, lines, RADIX, to_ref, high_ref, None, keep)
-    add_y(D1)
-    y_copy(U0).start()
-    add_z(D0)
-    start_z(D1)
+    add_y(DM)
+    start_z(DM)
+    y_copy(UM).start()
+    y_copy(U1).start()
     load_spectrum(2).wait()
     product(width, spectrum.at[0], wave_ref, True, high_ref, None)
 
@@ -1412,11 +1499,12 @@
         qkv_grad[2 * pair : 2 * pair + 2] = value.astype(jnp.bfloat16).reshape((2,) + qkv_grad.shape[1:])
     core_copy(QKV, 0).start()
     project_back(place.s * own_rows, put_own)
-    add_y(U0)
-    y_copy(U1).start()
+    add_y(UM)
+    start_z(UM)
     add_core(QKV)
-    add_z(D1)
-    start_z(U0)
+    y_copy(QKV).start()
+    add_y(U1)
+    start_z(U1)
     load_spectrum(3).wait()
     product(width, spectrum.at[1], wave_ref, True, high_ref, None)
     small_rows[...] = jnp.zeros(small_rows.shape, jnp.float32)
@@ -1424,19 +1512,20 @@
         width, TAP_ROWS, from_ref, high_ref, None
     )
     decay_gradients(0, length, ssm_ref, decay_ref, ssm_ref_all)
-    add_y(U1)
-    y_copy(QKV).start()
-    add_z(U0)
-    start_z(U1)
-    decay_gradients(1, length, ssm_ref, decay_ref, ssm_ref_all)
     add_y(QKV)
     start_z(QKV)
     y_copy(OUT).start()
+    add_z(D1)
+    add_z(DM)
+    decay_gradients(1, length, ssm_ref, decay_ref, ssm_ref_all)
+    add_z(UM)
     add_z(U1)
+    add_y(OUT)
+    start_z(OUT)
     decay_gradients(2, length, ssm_ref, decay_ref, ssm_ref_all)
     over_peers(lambda step: to_peer(ssm_ref_all, ssm_all, ss_s, ss_r, step).start())
     gn_copy.wait_recv()
-    for k in (D0, D1, U0, U1):
+    for k in (D1, DM, UM, U1):
         last_copy(k).start()
 
     def norm_back(index, sums):
@@ -1448,16 +1537,16 @@
         return sums[0] + gain, sums[1] + bias
 
     zero = jnp.sum(norm_two_ref[...], axis=0, keepdims=True) * 0.0
-    gain, bias = lax.fori_loop(0, own_rows // 32, norm_back, (zero, zero))
+    gain, bias = lax.fori_loop(0, own_rows // 32, norm_back, (zero, zero), unroll=4)
     small_rows[TAP_ROWS : TAP_ROWS + 1, :] = gain
     small_rows[TAP_ROWS + 1 : TAP_ROWS + 2, :] = bias
     small_rows[TAP_ROWS + 2 : TAP_ROWS + 4, :] = norm_two_ref[...]
     small_ref[...] = small_rows[...].T.astype(jnp.bfloat16).reshape(small_ref.shape)
     over_peers(lambda step: to_peer(small_ref, small_all, sm_s, sm_r, step).start())
-    add_y(OUT)
-    start_z(OUT)
     add_z(QKV)
     last_copy(QKV).start()
+    add_z(OUT)
+    last_copy(OUT).start()
 
     over_peers(lambda step: from_peer(ssm_all, ss_s, ss_r, step).wait_recv())
     ssm_all[place.d] = ssm_ref_all[place.d]
@@ -1473,8 +1562,6 @@
 
     small_sum[...] = lax.fori_loop(1, 16, add_small, small_ref[place.d].astype(jnp.float32)).astype(jnp.bfloat16)
     small_copy.start()
-    add_z(OUT)
-    last_copy(OUT).start()
     for k in range(count):
         finish(k)
     over_peers(lambda step: from_peer(ssm_sum, sg_s, sg_r, step).wait_recv())
@@ -1592,7 +1679,7 @@
 
 
 def adam_body(
-    down_first, up_last, down_last, out_sum, up_first, qkv_sum, small_sum, ssm_sum,
+    early_sum, down_last, up_last, down_next, up_next, out_sum, qkv_sum, small_sum, ssm_sum,
     attn_p, mlp_p, norm_p, tap_p, ssm_p, attn_m, mlp_m, norm_m, tap_m, ssm_m,
     attn_step, attn_new, mlp_step, mlp_new, norm_step, norm_new, tap_step, tap_new, ssm_step, ssm_new,
     *, scale,
@@ -1621,10 +1708,12 @@
         for place in range(3):
             attn((2 * place + half) * width, qkv_sum[half, :, place * width : (place + 1) * width])
         attn((6 + half) * width, out_sum[half])
-        mlp(0, up_first.shape[1] + half * up_last.shape[2], up_last, half)
-    mlp(0, 0, up_first, None)
-    mlp(1, 0, down_first, None)
-    mlp(1, down_first.shape[1], down_last, None)
+        mlp(0, up_last.shape[2] * 2 + half * up_last.shape[2], up_last, half)
+    for piece in range(early_sum.shape[0]):
+        mlp(1 - piece % 2, piece // 2 * HIDDEN_BLOCK, early_sum, piece)
+    mlp(0, HIDDEN_BLOCK, up_next, None)
+    mlp(1, HIDDEN_BLOCK, down_next, None)
+    mlp(1, down_last.shape[1], down_last, None)
     tap_step[...], tap_new[0], tap_new[1] = adam_parts(
         tap_p[...].astype(f32), tap_m[0], tap_m[1], small_sum[:, :TAP_ROWS] * scale, LEARN_RATE, DECAY_RATE
     )
@@ -1686,7 +1775,7 @@
     ssm_turned = jnp.swapaxes(ssm_params, 1, 2)
     (
         qkv_full, _, _, small_full, normed_low, query, value, conv, shifted, kernel_w, taps_w, keys_w, mixed_w,
-        layer_out, grad_residual, grad_norm_two, grad_gated, grad_up, grad_down, grad_out,
+        layer_out, grad_residual, grad_norm_two, grad_gated, grad_up, grad_down, grad_out, early_sums,
     ) = forward_layer(
         tokens[0], cotangent[0], attn_weight, mlp_weight, small, ssm_turned,
         to_table, from_table,
@@ -1700,7 +1789,7 @@
     (
         attn_step, attn_new, mlp_step, mlp_new, norms_step, norm_new, taps_step, tap_new, ssm_step, ssm_new
     ) = adam_all(
-        sums[:8],
+        (early_sums,) + tuple(sums[:8]),
         (attn_weight, mlp_weight, norms, taps.T, ssm_turned),
         (attn_moments, mlp_moments, norm_moments, turned_last(tap_moments), turned_last(ssm_moments)),
         scale,

time: 245 us -> 234 us (0.955)
  Pallas kernels: 239 us -> 228 us
    pallas_call x1, Pallas kernels: 109 us -> 92.2 us  [backward_mixer(): pl.pallas_call(backward_body, out_shape=tuple(results), in_specs=[vmem, a...]
    pallas_call x1, Pallas kernels: 124 us -> 129 us  [forward_layer(): pl.pallas_call(forward_body, out_shape=tuple((out for out, _ in outs)), i...]
where the time goes in v2:
time: 234 us
  Pallas kernels  228 us (97%)
  local copies, waits for them, and re-layouts  3.68 us (2%)
    pallas_call x1, Pallas kernels, forward_layer(): pl.pallas_call(forward_body, out_shape=tuple((out for out, _ in outs)), i...  129 us
    pallas_call x1, Pallas kernels, backward_mixer(): pl.pallas_call(backward_body, out_shape=tuple(results), in_specs=[vmem, a...  92.2 us
    pallas_call x1, Pallas kernels, adam_all(): pl.pallas_call(partial(adam_body, scale=scale), out_shape=tuple(outs), in...  6.17 us

profile of v2, /device:TPU:0, one launch (start us, length us, event | category | flops | bytes accessed | tf_op | source)
XLA Modules:
  0.0 233.5 jit_solution(18140982837598743452)
XLA Ops:
  0.7 0.1 pad.2.clone
  0.7 0.8 copy.26
  1.5 1.4 maximum_bitcast_fusion.small_ref
  2.9 129.4 %forward_layer.1 = (bf16[4,2,2,48,1152]{4,3,2,1,0:T(8,128)(2,1)}, bf16[4,2,2,48,3072]{4,3,2,1,0:T(8,128)(2,1)}, bf16[4,2,2,48,3072]{4,3,2,1,0:T(8,128)(2,1)}, f3...) custom-call(bf16[512,768]{1,0:T(8,128)(2,1)} %bitcast.15, ...), custom_call_target="tpu_custom_call" | custom-call | tf_op jit(solution)/shard_map/forward_layer/pallas_call | solution.py:1195
  132.3 92.2 %backward_mixer.1 = (f32[48,1536]{1,0:T(8,128)}, bf16[2,48,768]{2,1,0:T(8,128)(2,1)}, f32[48,768]{1,0:T(8,128)}, f32[48,768]{1,0:T(8,128)}, bf16[2,48,384]{2,1,0...) custom-call(bf16[2,512,384]{2,1,0:T(8,128)(2,1)} %get-tuple-element., ...), custom_call_target="tpu_custom_call" | custom-call | tf_op jit(solution)/shard_map/backward_mixer/pallas_call | solution.py:1620
  224.5 0.0 copy-start.1
  224.5 6.2 %adam.1 = (f32[48,3072]{1,0:T(8,128)}, f32[2,48,3072]{2,1,0:T(8,128)}, f32[2,48,3072]{2,1,0:T(8,128)}, f32[2,2,48,3072]{3,2,1,0:T(8,128)}, f32[4,48]{1,0:T(4,128...) custom-call(f32[2,48,768]{2,1,0:T(8,128)} %get-tuple-element.69.earl, ...), custom_call_target="tpu_custom_call" | custom-call | tf_op jit(solution)/shard_map/adam/pallas_call | solution.py:1736
  230.7 0.0 copy-start
  230.7 0.0 copy-done.1
  230.7 0.9 copy.29
  231.6 0.8 copy-done
  232.4 1.1 copy.30
  (1 shorter events, 0.0 us)
Async XLA Ops:
  224.5 6.2 %copy-start.1 = (bf16[512,768]{1,0:T(8,128)(2,1)S(1)}, bf16[512,768]{1,0:T(8,128)(2,1)}, u32[]{:S(2)}) copy-start(bf16[512,768]{1,0:T(8,128)(2,1)} %get-tuple-element.50) | copy-start | bytes 2359300
  230.7 1.7 copy-start

commit v3 on v2

--- a/solution.py
+++ b/solution.py
@@ -1043,10 +1043,10 @@
                 core_copy(DOWN_THIRD).wait_recv()
                 for copy in load(j):
                     copy.start()
+                early_y(1).start()
             if j == 3:
                 step_fourteen()
-                early_y(0).start()
-                early_y(1).start()
+                early_add_y(0)
                 core_copy(DOWN_LAST).wait_recv()
                 for copy in load(j):
                     copy.start()
@@ -1074,6 +1074,7 @@
             lax.fori_loop(0, own_rows // 256, rows_of, 0)
             if j == 1:
                 early_add_core(0)
+                early_y(0).start()
                 early_add_core(1)
             if j > EARLY:
                 for copy in store(j - 1):
@@ -1086,6 +1087,7 @@
             else:
                 for copy in store(j):
                     copy.start()
+        early_add_y(1)
 
         def norm_back(index, sums):
             rows = pl.ds(pl.multiple_of(index * 32, 32), 32)
@@ -1109,13 +1111,11 @@
         grad_copy.start()
         own_w = out_full[pl.ds(2 * place.s, 2)].reshape(width, model)
         gated_grad[place.s] = dot_right(active_ref[...], own_w).astype(low)
-        early_add_y(0)
-        early_add_y(1)
+        early_add_z(0)
         for h in range(2):
             out_grad[2 * h : 2 * h + 2] = dot_left(rows_ref[h], active_ref[...]).astype(low).reshape(part_shape)
         for copy in store(blocks - 1):
             copy.wait()
-        early_add_z(0)
         early_add_z(1)
         grad_copy.wait_recv()
         for e in range(2 * EARLY):
@@ -1253,7 +1253,7 @@
     count = len(PIECES)
     (
         grad_all, query_hbm, value_hbm, conv_ref, shifted_ref, kernel_w, taps_w, keys_w, mixed_w, ssm_ref, to_ref, from_ref,
-        normed_ref, qkv_ref, token_ref, residual_ref, small_t, norm_two_ref, down_ref, up_ref, out_ref,
+        normed_hbm, qkv_hbm, token_hbm, residual_hbm, small_t, norm_two_ref, down_ref, up_ref, out_ref,
     ), refs = refs[:21], refs[21:]
     outs, refs = refs[:count], refs[count:]
     (small_out, ssm_out, input_out), refs = refs[:3], refs[3:]
@@ -1263,12 +1263,12 @@
     from_y, from_z, final, last = (refs[i * count : (i + 1) * count] for i in range(4))
     refs = refs[4 * count :]
     (
-        own_ref, query_ref, value_ref, spectrum, line_ref, decay_ref, wave_ref, high_ref, back_ref,
+        normed_ref, qkv_ref, token_ref, residual_ref, own_ref, query_ref, value_ref, spectrum, line_ref, decay_ref, wave_ref, high_ref, back_ref,
         grad_proj, qkv_grad, gn_send, gn_own, gn_last, small_rows, small_ref, small_all, small_sum, small_last,
         ssm_ref_all, ssm_all, ssm_sum,
-    ), refs = refs[:22], refs[22:]
+    ), refs = refs[:26], refs[26:]
     (
-        load_sem, own_sem, core_s, core_r, x_s, x_r, y_s, y_r, z_s, z_r, f_s, f_r, sm_s, sm_r, ss_s, ss_r, sg_s, sg_r,
+        load_sem, late_sem, own_sem, core_s, core_r, x_s, x_r, y_s, y_r, z_s, z_r, f_s, f_r, sm_s, sm_r, ss_s, ss_r, sg_s, sg_r,
         side_s, side_r,
     ) = refs
     length, width = conv_ref.shape
@@ -1393,6 +1393,12 @@
     query_copy = pltpu.make_async_copy(query_hbm, query_ref, load_sem.at[2])
     value_copy = pltpu.make_async_copy(value_hbm, value_ref, load_sem.at[3])
 
+    late_copies = [
+        pltpu.make_async_copy(source, target, late_sem.at[i])
+        for i, (source, target) in enumerate(
+            ((qkv_hbm, qkv_ref), (normed_hbm, normed_ref), (token_hbm, token_ref), (residual_hbm, residual_ref))
+        )
+    ]
     greet_all(place)
     for k in range(QKV):
         for h in range(piece_halves(k)):
@@ -1403,6 +1409,8 @@
     load_spectrum(0).start()
     value_copy.start()
     load_spectrum(1).start()
+    for copy in late_copies:
+        copy.start()
     add_core(D1)
     y_copy(D1).start()
     load_own(DM)
@@ -1488,8 +1496,11 @@
     def put_own(rows, value):
         gn_own[rows, :] = value
 
+    late_copies[0].wait()
     project_back((1 - place.s) * own_rows, put_send)
     gn_copy.start()
+    for copy in late_copies[1:]:
+        copy.wait()
     for pair in range(TWO):
         columns = 2 * 4 * qkv_grad.shape[3]
         value = lax.dot_general(
@@ -1620,7 +1631,12 @@
     return pl.pallas_call(
         backward_body,
         out_shape=tuple(results),
-        in_specs=[vmem, anywhere, anywhere, vmem, vmem] + [anywhere] * 4 + [vmem] * 9 + [anywhere] * 3,
+        in_specs=[vmem, anywhere, anywhere, vmem, vmem]
+        + [anywhere] * 4
+        + [vmem] * 3
+        + [anywhere] * 4
+        + [vmem] * 2
+        + [anywhere] * 3,
         out_specs=(vmem,) * len(results),
         scratch_shapes=near
         + from_x
@@ -1629,6 +1645,10 @@
         + final
         + last
         + [
+            pltpu.VMEM((length, model), low),
+            pltpu.VMEM((model, 3 * width), low),
+            pltpu.VMEM((own_rows, model), low),
+            pltpu.VMEM((own_rows, model), f32),
             pltpu.VMEM((2, FOUR, TWO, owned, 1536), low),
             pltpu.VMEM((length, width), f32),
             pltpu.VMEM((length, width), f32),
@@ -1651,6 +1671,7 @@
             pltpu.VMEM(slots, f32),
             pltpu.VMEM(slots, f32),
             pltpu.VMEM(slots, f32),
+            dma((4,)),
             dma((4,)),
             dma((2, TWO)),
             dma((count, TWO)),

time: 234 us -> 228 us (0.974)
  Pallas kernels: 228 us -> 221 us
    pallas_call x1, Pallas kernels: 92.2 us -> 88.4 us  [backward_mixer(): pl.pallas_call(backward_body, out_shape=tuple(results), in_specs=[vmem, a...]
    pallas_call x1, Pallas kernels: 129 us -> 127 us  [forward_layer(): pl.pallas_call(forward_body, out_shape=tuple((out for out, _ in outs)), i...]
where the time goes in v3:
time: 228 us; the launch traced here: 227 us
  Pallas kernels  221 us (97%)
  local copies, waits for them, and re-layouts  3.68 us (2%)
    pallas_call x1, Pallas kernels, forward_layer(): pl.pallas_call(forward_body, out_shape=tuple((out for out, _ in outs)), i...  127 us
    pallas_call x1, Pallas kernels, backward_mixer(): pl.pallas_call(backward_body, out_shape=tuple(results), in_specs=[vmem, a...  88.4 us
    pallas_call x1, Pallas kernels, adam_all(): pl.pallas_call(partial(adam_body, scale=scale), out_shape=tuple(outs), in...  6.17 us

profile of v3, /device:TPU:0, one launch (start us, length us, event | category | flops | bytes accessed | tf_op | source)
XLA Modules:
  0.0 227.2 jit_solution(11040468958537497147)
XLA Ops:
  0.7 0.1 pad.2.clone
  0.7 0.8 copy.26
  1.5 1.4 maximum_bitcast_fusion.small_ref
  2.9 126.9 %forward_layer.1 = (bf16[4,2,2,48,1152]{4,3,2,1,0:T(8,128)(2,1)}, bf16[4,2,2,48,3072]{4,3,2,1,0:T(8,128)(2,1)}, bf16[4,2,2,48,3072]{4,3,2,1,0:T(8,128)(2,1)}, f3...) custom-call(bf16[512,768]{1,0:T(8,128)(2,1)} %bitcast.15, ...), custom_call_target="tpu_custom_call" | custom-call | tf_op jit(solution)/shard_map/forward_layer/pallas_call | solution.py:1195
  129.8 88.4 %backward_mixer.1 = (f32[48,1536]{1,0:T(8,128)}, bf16[2,48,768]{2,1,0:T(8,128)(2,1)}, f32[48,768]{1,0:T(8,128)}, f32[48,768]{1,0:T(8,128)}, bf16[2,48,384]{2,1,0...) custom-call(bf16[2,512,384]{2,1,0:T(8,128)(2,1)} %get-tuple-element., ...), custom_call_target="tpu_custom_call" | custom-call | tf_op jit(solution)/shard_map/backward_mixer/pallas_call | solution.py:1631
  218.2 0.0 copy-start.1
  218.2 6.2 %adam.1 = (f32[48,3072]{1,0:T(8,128)}, f32[2,48,3072]{2,1,0:T(8,128)}, f32[2,48,3072]{2,1,0:T(8,128)}, f32[2,2,48,3072]{3,2,1,0:T(8,128)}, f32[4,48]{1,0:T(4,128...) custom-call(f32[2,48,768]{2,1,0:T(8,128)} %get-tuple-element.69.earl, ...), custom_call_target="tpu_custom_call" | custom-call | tf_op jit(solution)/shard_map/adam/pallas_call | solution.py:1757
  224.3 0.0 copy-start
  224.4 0.0 copy-done.1
  224.4 0.9 copy.29
  225.2 0.8 copy-done
  226.0 1.1 copy.30
  (1 shorter events, 0.0 us)
Async XLA Ops:
  218.2 6.2 %copy-start.1 = (bf16[512,768]{1,0:T(8,128)(2,1)S(1)}, bf16[512,768]{1,0:T(8,128)(2,1)}, u32[]{:S(2)}) copy-start(bf16[512,768]{1,0:T(8,128)(2,1)} %get-tuple-element.50) | copy-start | bytes 2359300
  224.3 1.7 copy-start

commit v4 on v3

--- a/solution.py
+++ b/solution.py
@@ -656,11 +656,11 @@
 
 
 def forward_body(
-    token_ref, cotangent_ref, attn_shard, mlp_shard, small_ref, ssm_ref, to_ref, from_ref,
+    token_ref, cotangent_hbm, attn_shard, mlp_shard, small_ref, ssm_ref, to_hbm, from_hbm,
     qkv_full, up_full, down_full, small_t, normed_ref, query_out, value_out, conv_ref, shifted_ref,
     kernel_out, taps_out, keys_out, mixed_out, layer_out, residual_grad, norm_two_out, gated_grad, up_grad, down_grad, out_grad, early_out,
-    qkv_ref, token_all, small_all, gated_ref, rows_ref, out_full, grad_send, near, from_y, from_z, final, last,
-    own_sem, z_s, z_r, y_s, y_r, x_s, x_r, core_s, core_r, small_s, small_r, side_s, side_r, store_sem, load_sem, nc_s, nc_r, ny_s, ny_r, nz_s, nz_r, nf_s, nf_r,
+    cotangent_ref, to_ref, from_ref, qkv_ref, token_all, small_all, gated_ref, rows_ref, out_full, grad_send, near, from_y, from_z, final, last,
+    own_sem, z_s, z_r, y_s, y_r, x_s, x_r, core_s, core_r, small_s, small_r, side_s, side_r, store_sem, load_sem, nc_s, nc_r, ny_s, ny_r, nz_s, nz_r, nf_s, nf_r, late_sem,
 ):
     length, width = conv_ref.shape
     own_rows, model = token_ref.shape
@@ -841,8 +841,14 @@
     for j in range(3):
         cols = pl.ds(pl.multiple_of((2 * j + place.s) * width, LANES), width)
         qkv_ref[:, j * width : (j + 1) * width] = attn_shard[:, cols]
+    late_copies = [
+        pltpu.make_async_copy(source, target, late_sem.at[i])
+        for i, (source, target) in enumerate(((to_hbm, to_ref), (from_hbm, from_ref), (cotangent_hbm, cotangent_ref)))
+    ]
     greet_all(place)
     start_z(QKV_W)
+    for copy in late_copies:
+        copy.start()
     over_peers(lambda step: small_copy(step).start())
     token_copy.start()
     for copy in own_copies():
@@ -876,6 +882,8 @@
             if not block:
                 start_z(OUT_W)
         step_one()
+        for copy in late_copies:
+            copy.wait()
         to_waves(width, lines, RADIX, to_ref, high_ref, low_ref, keep(kernel_w))
         stores[0].start()
         over_peers(lambda step: small_arrival(step).wait_recv())
@@ -1195,9 +1203,12 @@
     return pl.pallas_call(
         forward_body,
         out_shape=tuple(out for out, _ in outs),
-        in_specs=[vmem, vmem, vmem, anywhere, vmem, vmem, vmem, vmem],
+        in_specs=[vmem, anywhere, vmem, anywhere, vmem, vmem, anywhere, anywhere],
         out_specs=tuple(spec for _, spec in outs),
         scratch_shapes=[
+            pltpu.VMEM(cotangent.shape, low),
+            pltpu.VMEM(to_table.shape, low),
+            pltpu.VMEM(from_table.shape, low),
             pltpu.VMEM((owned, 3 * width), low),
             pltpu.VMEM((2, own_rows, model), low),
             pltpu.VMEM((16,) + small.shape, low),
@@ -1228,7 +1239,8 @@
         ]
         + [dma((2 * EARLY,))] * 4
         + [dma((2 * EARLY, 3))] * 2
-        + [dma((2 * EARLY,))] * 2,
+        + [dma((2 * EARLY,))] * 2
+        + [dma((3,))],
         compiler_params=pltpu.CompilerParams(collective_id=2, has_side_effects=True, vmem_limit_bytes=VMEM_LIMIT),
         name="forward_layer",
     )(tokens, cotangent, attn_shard, mlp_shard, small, ssm, to_table, from_table)
@@ -1252,7 +1264,7 @@
 def backward_body(*refs):
     count = len(PIECES)
     (
-        grad_all, query_hbm, value_hbm, conv_ref, shifted_ref, kernel_w, taps_w, keys_w, mixed_w, ssm_ref, to_ref, from_ref,
+        grad_all, query_hbm, value_hbm, conv_ref, shifted_ref, kernel_w, taps_w, keys_w, mixed_w, ssm_ref, to_hbm, from_hbm,
         normed_hbm, qkv_hbm, token_hbm, residual_hbm, small_t, norm_two_ref, down_ref, up_ref, out_ref,
     ), refs = refs[:21], refs[21:]
     outs, refs = refs[:count], refs[count:]
@@ -1263,10 +1275,10 @@
     from_y, from_z, final, last = (refs[i * count : (i + 1) * count] for i in range(4))
     refs = refs[4 * count :]
     (
-        normed_ref, qkv_ref, token_ref, residual_ref, own_ref, query_ref, value_ref, spectrum, line_ref, decay_ref, wave_ref, high_ref, back_ref,
+        to_ref, from_ref, normed_ref, qkv_ref, token_ref, residual_ref, own_ref, query_ref, value_ref, spectrum, line_ref, decay_ref, wave_ref, high_ref, back_ref,
         grad_proj, qkv_grad, gn_send, gn_own, gn_last, small_rows, small_ref, small_all, small_sum, small_last,
         ssm_ref_all, ssm_all, ssm_sum,
-    ), refs = refs[:26], refs[26:]
+    ), refs = refs[:28], refs[28:]
     (
         load_sem, late_sem, own_sem, core_s, core_r, x_s, x_r, y_s, y_r, z_s, z_r, f_s, f_r, sm_s, sm_r, ss_s, ss_r, sg_s, sg_r,
         side_s, side_r,
@@ -1399,6 +1411,8 @@
             ((qkv_hbm, qkv_ref), (normed_hbm, normed_ref), (token_hbm, token_ref), (residual_hbm, residual_ref))
         )
     ]
+    to_copy = pltpu.make_async_copy(to_hbm, to_ref, late_sem.at[4])
+    from_copy = pltpu.make_async_copy(from_hbm, from_ref, late_sem.at[5])
     greet_all(place)
     for k in range(QKV):
         for h in range(piece_halves(k)):
@@ -1406,6 +1420,8 @@
     load_own(D1)
     load_own(U1)
     query_copy.start()
+    to_copy.start()
+    from_copy.start()
     load_spectrum(0).start()
     value_copy.start()
     load_spectrum(1).start()
@@ -1438,6 +1454,8 @@
         return (gradient * query_ref[rows, cols]).astype(jnp.bfloat16).astype(jnp.float32)
 
     query_copy.wait()
+    to_copy.wait()
+    from_copy.wait()
     value_copy.wait()
     to_waves(width, read_conv_grad, RADIX, to_ref, high_ref, None, keep)
     load_spectrum(0).wait()
@@ -1633,8 +1651,8 @@
         out_shape=tuple(results),
         in_specs=[vmem, anywhere, anywhere, vmem, vmem]
         + [anywhere] * 4
-        + [vmem] * 3
-        + [anywhere] * 4
+        + [vmem]
+        + [anywhere] * 6
         + [vmem] * 2
         + [anywhere] * 3,
         out_specs=(vmem,) * len(results),
@@ -1645,6 +1663,8 @@
         + final
         + last
         + [
+            pltpu.VMEM(to_table.shape, low),
+            pltpu.VMEM(from_table.shape, low),
             pltpu.VMEM((length, model), low),
             pltpu.VMEM((model, 3 * width), low),
             pltpu.VMEM((own_rows, model), low),
@@ -1672,7 +1692,7 @@
             pltpu.VMEM(slots, f32),
             pltpu.VMEM(slots, f32),
             dma((4,)),
-            dma((4,)),
+            dma((6,)),
             dma((2, TWO)),
             dma((count, TWO)),
             dma((count, TWO)),

time: 228 us -> 225 us (0.987)
  no operation moved by 1% of the time
where the time goes in v4:
time: 225 us
  Pallas kernels  219 us (97%)
  local copies, waits for them, and re-layouts  3.68 us (2%)
    pallas_call x1, Pallas kernels, forward_layer(): pl.pallas_call(forward_body, out_shape=tuple((out for out, _ in outs)), i...  125 us
    pallas_call x1, Pallas kernels, backward_mixer(): pl.pallas_call(backward_body, out_shape=tuple(results), in_specs=[vmem, a...  87.5 us
    pallas_call x1, Pallas kernels, adam_all(): pl.pallas_call(partial(adam_body, scale=scale), out_shape=tuple(outs), in...  6.17 us

profile of v4, /device:TPU:0, one launch (start us, length us, event | category | flops | bytes accessed | tf_op | source)
XLA Modules:
  0.0 224.5 jit_solution(12106616549546960155)
XLA Ops:
  0.7 0.1 pad.2.clone
  0.7 0.8 copy.26
  1.5 1.4 maximum_bitcast_fusion.small_ref
  2.9 125.1 %forward_layer.1 = (bf16[4,2,2,48,1152]{4,3,2,1,0:T(8,128)(2,1)}, bf16[4,2,2,48,3072]{4,3,2,1,0:T(8,128)(2,1)}, bf16[4,2,2,48,3072]{4,3,2,1,0:T(8,128)(2,1)}, f3...) custom-call(bf16[512,768]{1,0:T(8,128)(2,1)} %bitcast.15, ...), custom_call_target="tpu_custom_call" | custom-call | tf_op jit(solution)/shard_map/forward_layer/pallas_call | solution.py:1203
  128.0 87.5 %backward_mixer.1 = (f32[48,1536]{1,0:T(8,128)}, bf16[2,48,768]{2,1,0:T(8,128)(2,1)}, f32[48,768]{1,0:T(8,128)}, f32[48,768]{1,0:T(8,128)}, bf16[2,48,384]{2,1,0...) custom-call(bf16[2,512,384]{2,1,0:T(8,128)(2,1)} %get-tuple-element., ...), custom_call_target="tpu_custom_call" | custom-call | tf_op jit(solution)/shard_map/backward_mixer/pallas_call | solution.py:1649
  215.5 0.0 copy-start.1
  215.5 6.2 %adam.1 = (f32[48,3072]{1,0:T(8,128)}, f32[2,48,3072]{2,1,0:T(8,128)}, f32[2,48,3072]{2,1,0:T(8,128)}, f32[2,2,48,3072]{3,2,1,0:T(8,128)}, f32[4,48]{1,0:T(4,128...) custom-call(f32[2,48,768]{2,1,0:T(8,128)} %get-tuple-element.69.earl, ...), custom_call_target="tpu_custom_call" | custom-call | tf_op jit(solution)/shard_map/adam/pallas_call | solution.py:1777
  221.7 0.0 copy-start
  221.7 0.0 copy-done.1
  221.7 0.9 copy.29
  222.6 0.8 copy-done
  223.4 1.1 copy.30
  (1 shorter events, 0.0 us)
Async XLA Ops:
  215.5 6.2 %copy-start.1 = (bf16[512,768]{1,0:T(8,128)(2,1)S(1)}, bf16[512,768]{1,0:T(8,128)(2,1)}, u32[]{:S(2)}) copy-start(bf16[512,768]{1,0:T(8,128)(2,1)} %get-tuple-element.50) | copy-start | bytes 2359300
  221.7 1.7 copy-start
